TPU v7x, 256 devices: a whole 4x4x8 slice. The times are simulated.
256 devices in a mesh: ctx: 64 (over x, z, core), lat: 4 (over y).
Axes of the slice: x: 4, y: 4, z: 8, core: 2. Of those that a mesh axis runs over, the one named last changes fastest.
Arguments:
- token_ids: int32 [32768], P('ctx'), may hold values from 0 to 255
- latent_offset: int32 [1], replicated, may hold values from 31616 to 31744
- embed_table: bfloat16 [256, 2048], replicated, may hold values from -6 to 6
- cross_q: bfloat16 [2048, 2048], P('ctx', 'lat')
- cross_kv: bfloat16 [2, 2048, 2048], P(None, 'ctx', 'lat')
- cross_out: bfloat16 [2048, 2048], P('lat'), may hold values from -0.375 to 0.375
- self_qkv: bfloat16 [3, 2048, 2048], P(None, None, 'lat')
- self_out: bfloat16 [2048, 2048], P('lat'), may hold values from -0.25 to 0.25
- mlp_in: bfloat16 [2048, 8192], P(None, 'ctx'), may hold values from -0.125 to 0.125
- mlp_out: bfloat16 [8192, 2048], P('ctx'), may hold values from -0.0625 to 0.0625
Outputs:
- latent_out: bfloat16 [4, 256, 2048], P('lat', 'ctx')
Inputs may be any that keep to these rules, and one draw needn't show every extreme that they name: `latent_offset`: the latent rows lie inside the context.
All inputs are finite; a program needn't handle non-finite values.
Results may differ from a plain program's by a relative error of at most 0.014.
Values may be sent and summed in bfloat16 or wider, within the bound.
A program may use at most 128 MiB of HBM per device.

v0:
```python
import math

import jax
import jax.numpy as jnp
from jax import lax
from jax.sharding import PartitionSpec as P

HD = 128
LATENTS = 1024


EPSILON = 1e-06
MASKED = -1e30


def sent_to_all(array, axis):
    count = lax.axis_size(axis)
    return lax.all_to_all(
        jnp.broadcast_to(array[None], (count, *array.shape)), axis, 0, 0, tiled=True
    )


def laid_out(pieces, dim):
    pieces = jnp.moveaxis(pieces, 0, dim)
    shape = pieces.shape
    return pieces.reshape(*shape[:dim], shape[dim] * shape[dim + 1], *shape[dim + 2 :])


def gathered_copies(array, axis, dim):
    pieces = sent_to_all(array, axis)
    return laid_out(pieces, dim)


def side_by_side(arrays, axis, split_dim, concat_dim, along):
    ends, at = ([], 0)
    for a in arrays[:-1]:
        at += a.shape[along]
        ends.append(at)
    both = jnp.concatenate(arrays, axis=along)
    return tuple(
        jnp.split(
            lax.all_to_all(both, axis, split_axis=split_dim, concat_axis=concat_dim, tiled=True),
            ends,
            axis=along,
        )
    )


def of_everyone(array, axis):
    return sent_to_all(array, axis).sum(axis=0)


def side_by_side_2(arrays, axis, dim, along):
    ends, at = ([], 0)
    for a in arrays[:-1]:
        at += a.shape[along]
        ends.append(at)
    both = jnp.concatenate(arrays, axis=along)
    return tuple(jnp.split(lax.all_gather(both, axis, axis=dim, tiled=True), ends, axis=along))


def over_copies(array, axis):
    everything = sent_to_all(array, axis)
    return jnp.sum(everything.astype(jnp.float32), axis=0)


def in_blocks(array, dim, count):
    before, after = (array.shape[:dim], array.shape[dim + 1 :])
    return jnp.moveaxis(array.reshape(*before, count, -1, *after), dim, 0)


def sent_and_summed(array, axis, dim):
    count = lax.axis_size(axis)
    pieces = lax.all_to_all(in_blocks(array, dim, count), axis, 0, 0, tiled=True)
    return jnp.sum(pieces, axis=0)


def rms_normalize(values):
    return values * lax.rsqrt(jnp.mean(values * values, axis=-1, keepdims=True) + EPSILON)


def sinusoid(places, width):
    index = jnp.arange(width // 2).astype(jnp.float32)
    rates = jnp.exp(index * (-2.0 * math.log(10000.0) / width))
    angles = places.astype(jnp.float32)[:, None] * rates[None, :]
    return jnp.stack([jnp.sin(angles), jnp.cos(angles)], axis=-1).reshape(places.shape[0], width)


def embed_rows(token_rows, table, places):
    vocab_range = jnp.arange(table.shape[0], dtype=jnp.int32)
    one_hot = (token_rows[:, None] == vocab_range[None, :]).astype(jnp.bfloat16)
    looked = jnp.dot(one_hot, table, preferred_element_type=jnp.float32)
    return rms_normalize(looked + sinusoid(places, table.shape[1])).astype(jnp.bfloat16)


def block_attention(queries, keys, values, blocked, head_size):
    scale = 1.0 / math.sqrt(head_size)
    head_count = queries.shape[1] // head_size
    query_rows = queries.shape[0]
    key_rows = keys.shape[0]
    query_heads = jnp.transpose(queries.reshape(query_rows, head_count, head_size), (1, 0, 2))
    key_heads = jnp.transpose(keys.reshape(key_rows, head_count, head_size), (1, 0, 2))
    value_heads = jnp.transpose(values.reshape(key_rows, head_count, head_size), (1, 0, 2))

    def one_head(operands):
        query, key, value = operands
        scores = (
            lax.dot_general(
                query, key, (((1,), (1,)), ((), ())), preferred_element_type=jnp.float32
            )
            * scale
        )
        scores = jnp.where(blocked, MASKED, scores)
        peak = jnp.max(scores, axis=1)
        weights = jnp.exp(scores - peak[:, None]).astype(jnp.bfloat16)
        total = jnp.sum(weights.astype(jnp.float32), axis=1)
        output = jnp.dot(weights, value, preferred_element_type=jnp.float32)
        return (peak, total, output)

    maxima, totals, outputs = lax.map(one_head, (query_heads, key_heads, value_heads))
    merged = jnp.transpose(outputs, (1, 0, 2)).reshape(query_rows, head_count * head_size)
    return (jnp.transpose(maxima), jnp.transpose(totals), merged)


def per_device(
    token_ids,
    latent_offset,
    embed_table,
    cross_q,
    cross_kv,
    cross_out,
    self_qkv,
    self_out,
    mlp_in,
    mlp_out,
):
    context_count = lax.axis_size("ctx")
    group_count = lax.axis_size("lat")
    context_index = lax.axis_index("ctx")
    group_index = lax.axis_index("lat")
    block_length = token_ids.shape[0]
    head_size = HD
    local_width = cross_q.shape[1]
    local_heads = local_width // head_size
    width = embed_table.shape[1]
    offset = latent_offset[0]
    latent_count = LATENTS
    row_count = latent_count // context_count
    group_rows = latent_count // group_count
    places = context_index * block_length + jnp.arange(block_length, dtype=jnp.int32)
    context = embed_rows(token_ids, embed_table, places)
    piece = lax.all_gather(cross_kv, "ctx", axis=1, tiled=True)
    columns = context
    key_sum = jnp.dot(columns, piece[0], preferred_element_type=jnp.float32)
    value_sum = jnp.dot(columns, piece[1], preferred_element_type=jnp.float32)
    keys = key_sum.astype(jnp.bfloat16)
    values = value_sum.astype(jnp.bfloat16)
    every_token = gathered_copies(token_ids, "ctx", 0)
    latent_tokens = lax.dynamic_slice_in_dim(every_token, offset, latent_count, 0)
    latent_places = offset + jnp.arange(latent_count, dtype=jnp.int32)
    latent = embed_rows(latent_tokens, embed_table, latent_places)
    columns = latent
    query_sum = jnp.dot(
        columns, gathered_copies(cross_q, "ctx", 0), preferred_element_type=jnp.float32
    )
    queries = query_sum.astype(jnp.bfloat16)
    blocked = places[None, :] > latent_places[:, None]
    maxima, totals, outputs = block_attention(queries, keys, values, blocked, head_size)
    row_start = context_index * row_count
    came_max, came_total, came_out = side_by_side(
        (maxima[:, None, :], totals[:, None, :], outputs[:, None, :]), "ctx", 0, 1, 2
    )
    peak = jnp.max(came_max, axis=1, keepdims=True)
    factor = jnp.exp(came_max - peak)
    own_totals = jnp.sum(came_total * factor, axis=1)
    spread = (
        came_out.reshape(row_count, context_count, local_heads, head_size) * factor[:, :, :, None]
    )
    own_outputs = jnp.sum(spread, axis=1).reshape(row_count, local_width)
    attended = (own_outputs / jnp.repeat(own_totals, head_size, axis=1)).astype(jnp.bfloat16)
    own_latent = lax.dynamic_slice_in_dim(latent, row_start, row_count, 0).astype(jnp.float32)
    first_stream = own_latent + of_everyone(
        jnp.dot(attended, cross_out, preferred_element_type=jnp.float32), "lat"
    )
    self_normed = rms_normalize(first_stream).astype(jnp.bfloat16)
    self_queries = jnp.dot(self_normed, self_qkv[0], preferred_element_type=jnp.float32).astype(
        jnp.bfloat16
    )
    self_keys = jnp.dot(self_normed, self_qkv[1], preferred_element_type=jnp.float32).astype(
        jnp.bfloat16
    )
    self_values = jnp.dot(self_normed, self_qkv[2], preferred_element_type=jnp.float32).astype(
        jnp.bfloat16
    )
    all_keys, all_values = side_by_side_2((self_keys, self_values), "ctx", 0, 1)
    own_places = row_start + jnp.arange(row_count, dtype=jnp.int32)
    later = jnp.arange(latent_count, dtype=jnp.int32)[None, :] > own_places[:, None]
    self_peak, self_totals, self_outputs = block_attention(
        self_queries, all_keys, all_values, later, head_size
    )
    self_attended = (self_outputs / jnp.repeat(self_totals, head_size, axis=1)).astype(jnp.bfloat16)
    second_stream = first_stream + over_copies(
        jnp.dot(self_attended, self_out, preferred_element_type=jnp.float32).astype(jnp.bfloat16),
        "lat",
    ).astype(jnp.float32)
    mlp_normed = rms_normalize(second_stream).astype(jnp.bfloat16)
    gathered = lax.all_gather(mlp_normed, "ctx", axis=0, tiled=True)
    group_input = lax.dynamic_slice_in_dim(gathered, group_index * group_rows, group_rows, 0)
    pre_hidden = jnp.dot(group_input, mlp_in, preferred_element_type=jnp.float32)
    hidden = jax.nn.gelu(pre_hidden, approximate=True).astype(jnp.bfloat16)
    place = context_index * row_count - group_index * group_rows
    inside = jnp.logical_and(place >= 0, place < group_rows)
    residual = jnp.zeros((group_rows, width), jnp.float32)
    residual = lax.dynamic_update_slice_in_dim(
        residual, second_stream, jnp.clip(place, 0, group_rows - row_count), 0
    )
    residual = jnp.where(inside, residual, 0.0)
    result = sent_and_summed(
        jnp.dot(hidden, mlp_out, preferred_element_type=jnp.float32) + residual, "ctx", 0
    )
    return result.astype(jnp.bfloat16)[None]


def solution(mesh):
    placed = (
        P("ctx"),
        P(),
        P(),
        P("ctx", "lat"),
        P(None, "ctx", "lat"),
        P("lat", None),
        P(None, None, "lat"),
        P("lat", None),
        P(None, "ctx"),
        P("ctx", None),
    )
    return jax.shard_map(
        per_device, mesh=mesh, in_specs=placed, out_specs=P("lat", "ctx", None), check_vma=False
    )
```

profile of v0, /device:TPU:1, one launch (start us, length us, event | category | flops | bytes accessed | tf_op | source)
XLA Modules:
  0.0 527.7 jit_solution(14020587515841500525)
XLA Ops:
  8.0 23.1 %all_to_all.44 = s32[64,1,512]{2,1,0:T(1,128)S(1)} all-to-all(s32[64,1,512]{2,1,0:T(1,128)S(1)} %broadcast_in_dim.52), channel_id=1, replica_groups=mesh['ctx'=64,'lat'=4] {'ctx'}, dimensions={0} | all-to-all | bytes 262144 | tf_op jit(solution)/shard_map/all_to_all | solution.py:18
  33.6 6.0 %all-to-all-start.1 = ((bf16[64,32,512]{2,1,0:T(8,128)(2,1)}), bf16[64,32,512]{2,1,0:T(8,128)(2,1)}, u32[]{:S(2)}, u32[]{:S(2)}) async-start(bf16[64,32,512]{2,1,0:T(8,128)(2,1)} %broadcast_in_dim.54), calls=%async_computation.1 | async-start | bytes 4194304 | tf_op jit(solution)/shard_map/all_to_all | solution.py:18
  40.3 14.9 %multiply_sine_fusion = (f32[1024,1024,1]{1,0,2:T(8,128)S(1)}, f32[1024,1024,1]{1,0,2:T(8,128)S(1)}) fusion(f32[1024]{0:T(1024)S(1)} %multiply_exponential_fusion, f32[1024]{0:T(1024)S(1)} %get-tuple-element.184), kind=kLoop, calls=%fused_computation.36 | loop fusion | flops 1048576 | bytes 8396800 | tf_op jit(solution)/shard_map/sin | solution.py:86
  55.2 4.1 pad_maximum_fusion
  59.3 13.5 %copy.62 = f32[1024,1024,2]{0,2,1:T(2,128)} copy(f32[1024,1024,2]{1,0,2:T(8,128)} %pad_maximum_fusion) | data formatting | bytes 16777216 | tf_op jit(solution)/shard_map/stack | solution.py:86
  72.7 11.0 %reshape.308 = f32[1024,2048]{0,1:T(8,128)} reshape(f32[1024,1024,2]{0,2,1:T(2,128)} %copy.62) | data formatting | bytes 16777216 | tf_op jit(solution)/shard_map/reshape | solution.py:86
  83.7 9.3 %copy.63 = f32[1024,2048]{1,0:T(8,128)} copy(f32[1024,2048]{0,1:T(8,128)} %reshape.308) | data formatting | bytes 16777216 | tf_op jit(solution)/shard_map/reshape | solution.py:86
  93.0 7.3 %multiply_sine_fusion.1 = (f32[512,1024,1]{1,0,2:T(8,128)S(1)}, f32[512,1024,1]{1,0,2:T(8,128)S(1)}) fusion(f32[1024]{0:T(1024)S(1)} %multiply_exponential_fusion, f32[512]{0:T(512)S(1)} %get-tuple-element.186), kind=kLoop, calls=%fused_computation.43 | loop fusion | flops 524288 | bytes 4200448 | tf_op jit(solution)/shard_map/sin | solution.py:86
  102.7 7.3 %copy.65 = f32[512,1024,2]{0,2,1:T(2,128)} copy(f32[512,1024,2]{1,0,2:T(8,128)} %pad_maximum_fusion.1) | data formatting | bytes 8388608 | tf_op jit(solution)/shard_map/stack | solution.py:86
  109.9 6.1 %reshape.311 = f32[512,2048]{0,1:T(8,128)} reshape(f32[512,1024,2]{0,2,1:T(2,128)} %copy.65) | data formatting | bytes 8388608 | tf_op jit(solution)/shard_map/reshape | solution.py:86
  116.0 5.5 %copy.66 = f32[512,2048]{1,0:T(8,128)} copy(f32[512,2048]{0,1:T(8,128)} %reshape.311) | data formatting | bytes 8388608 | tf_op jit(solution)/shard_map/reshape | solution.py:86
  121.5 4.9 multiply_reduce_fusion.1
  126.5 4.6 multiply_reduce_fusion
  133.6 5.2 convolution_convert_fusion.1
  140.2 4.2 fusion.38
  144.7 5.1 fusion.37
  151.1 13.3 %while.28 = (s32[]{:T(128)}, f32[4,1024]{1,0:T(4,128)S(1)}, f32[4,1024]{1,0:T(4,128)S(1)}, f32[4,1024,128]{1,2,0:T(8,128)}, bf16[4,1024,128]{2,1,0:T(8,128)(2,1)...) while((s32[]{:T(128)}, f32[4,1024]{1,0:T(4,128)S(1)}, ...), condition=%wide.region_5.6_spmd.clone, body=%wide.region_2.5_spmd.clone.sunk | while | flops 274200576 | bytes 7383157 | solution.py:120
  164.4 3.3 pad_maximum_fusion.2
  167.7 6.3 %copy.70 = f32[1024,1,520]{2,1,0:T(1,128)} copy(f32[1024,1,520]{0,2,1:T(8,128)} %pad_maximum_fusion.2) | data formatting | bytes 4259840 | tf_op jit(solution)/shard_map/concatenate | solution.py:39
  173.9 72.6 %all_to_all.45 = f32[1024,1,520]{2,1,0:T(1,128)S(1)} all-to-all(f32[1024,1,520]{2,1,0:T(1,128)} %copy.70), channel_id=1, replica_groups=mesh['ctx'=64,'lat'=4] {'ctx'}, dimensions={0} | all-to-all | bytes 4259840 | tf_op jit(solution)/shard_map/all_to_all | solution.py:42
  250.7 3.1 mul.170
  253.8 3.0 fusion.25
  258.1 4.4 all-to-all-start.3
  262.5 9.2 %all-to-all-done.3 = f32[4,16,2048]{2,1,0:T(8,128)S(1)} async-done(((f32[4,16,2048]{2,1,0:T(8,128)}), f32[4,16,2048]{2,1,0:T(8,128)S(1)}, u32[]{:S(2)}, u32[]{:S(2)}) %all-to-all-start.3) | async-done | bytes 524320 | tf_op jit(solution)/shard_map/all_to_all | solution.py:18
  280.5 71.2 %all-gather.6.cloned.1.call-done = bf16[1024,1024]{1,0:T(8,128)(2,1)} async-done(((bf16[16,1024]{1,0:T(8,128)(2,1)}), bf16[1024,1024]{1,0:T(8,128)(2,1)}) %all-gather.6.cloned.1.call-update) | async-done | bytes 2097168 | tf_op jit(solution)/shard_map/all_gather | solution.py:59
  354.9 6.8 %while.29 = (s32[]{:T(128)}, f32[4,16]{1,0:T(4,128)S(1)}, f32[4,16,128]{2,1,0:T(8,128)S(1)}, bf16[4,16,128]{2,1,0:T(8,128)(2,1)S(1)}, bf16[4,1024,128]{2,1,0:T(8...) while((s32[]{:T(128)}, f32[4,16]{1,0:T(4,128)S(1)}, ...), condition=%wide.region_14.15_spmd.clone, body=%wide.region_11.14_spmd.clone.sunk | while | flops 8552418 | bytes 736673 | solution.py:120
  363.9 10.1 %all_to_all.46 = bf16[4,16,2048]{2,1,0:T(8,128)(2,1)S(1)} all-to-all(bf16[4,16,2048]{2,1,0:T(8,128)(2,1)S(1)} %broadcast_in_dim.106), channel_id=1, replica_groups=mesh['ctx'=64,'lat'=4] {'lat'}, dimensions={0} | all-to-all | bytes 524288 | tf_op jit(solution)/shard_map/all_to_all | solution.py:18
  375.7 76.2 %all-gather.8.cloned.1.call-done = bf16[1024,2048]{1,0:T(8,128)(2,1)} async-done(((bf16[16,2048]{1,0:T(8,128)(2,1)}), bf16[1024,2048]{1,0:T(8,128)(2,1)}) %all-gather.8.cloned.1.call-update) | async-done | bytes 4194320 | tf_op jit(solution)/shard_map/all_gather | solution.py:207
  451.9 3.5 fusion.69
  458.0 2.9 reshape.318
  460.9 57.5 %all_to_all.47 = f32[64,4,2048]{2,1,0:T(4,128)} all-to-all(f32[64,4,2048]{2,1,0:T(4,128)} %reshape.318), channel_id=1, replica_groups=mesh['ctx'=64,'lat'=4] {'ctx'}, dimensions={0} | all-to-all | bytes 4194304 | tf_op jit(solution)/shard_map/all_to_all | solution.py:74
  518.4 2.5 reduce_sum.107
  (100 shorter events, 55.5 us)
Async XLA Ops:
  6.5 250.4 %copy-start = (bf16[512,2048]{1,0:T(8,128)(2,1)S(1)}, bf16[512,2048]{1,0:T(8,128)(2,1)}, u32[]{:S(2)}) copy-start(bf16[512,2048]{1,0:T(8,128)(2,1)} %param.19) | copy-start | bytes 6291460
  6.5 133.6 %all-gather.4.cloned.1.call-start = ((), (), s32[]{:S(2)}) async-start(), calls=%async_computation.6 | async-start | bytes 4259840 | tf_op jit(solution)/shard_map/all_gather | solution.py:152
  33.6 100.0 %all-to-all-start.1 = ((bf16[64,32,512]{2,1,0:T(8,128)(2,1)}), bf16[64,32,512]{2,1,0:T(8,128)(2,1)}, u32[]{:S(2)}, u32[]{:S(2)}) async-start(bf16[64,32,512]{2,1,0:T(8,128)(2,1)} %broadcast_in_dim.54), calls=%async_computation.1 | async-start | bytes 4194304 | tf_op jit(solution)/shard_map/all_to_all | solution.py:18
  116.0 5.5 %copy-start.2 = (bf16[256,2048]{1,0:T(8,128)(2,1)S(1)}, bf16[256,2048]{1,0:T(8,128)(2,1)}, u32[]{:S(2)}) copy-start(bf16[256,2048]{1,0:T(8,128)(2,1)} %param.16) | copy-start | bytes 3145732
  116.0 5.5 %copy-start.4 = (s32[512]{0:T(512)S(1)}, s32[512]{0:T(512)}, u32[]{:S(2)}) copy-start(s32[512]{0:T(512)} %param.14) | copy-start | bytes 6148
  246.7 1.5 copy-start.1
  258.1 13.5 %all-to-all-start.3 = ((f32[4,16,2048]{2,1,0:T(8,128)}), f32[4,16,2048]{2,1,0:T(8,128)S(1)}, u32[]{:S(2)}, u32[]{:S(2)}) async-start(f32[4,16,2048]{2,1,0:T(8,128)} %broadcast_in_dim.58), calls=%async_computation.3 | async-start | bytes 1048576 | tf_op jit(solution)/shard_map/all_to_all | solution.py:18
  262.5 89.2 %all-gather.6.cloned.1.call-start = ((), (), s32[]{:S(2)}) async-start(), calls=%async_computation.7 | async-start | bytes 2129920 | tf_op jit(solution)/shard_map/all_gather | solution.py:59
  278.2 173.7 %all-gather.8.cloned.1.call-start = ((), (), s32[]{:S(2)}) async-start(), calls=%async_computation.8 | async-start | bytes 4259840 | tf_op jit(solution)/shard_map/all_gather | solution.py:207
  361.8 90.2 %copy-start.3 = (bf16[128,2048]{1,0:T(8,128)(2,1)S(1)}, bf16[128,2048]{1,0:T(8,128)(2,1)}, u32[]{:S(2)}) copy-start(bf16[128,2048]{1,0:T(8,128)(2,1)} %param.23) | copy-start | bytes 1572868
Sparse Core Ops, SparseCore 0:
  10.2 92.9 all-gather.3
  278.3 73.3 all-gather.5
  375.8 76.0 all-gather.7
where the time goes:
time: 533 us; the launch traced here: 528 us
  blocking collectives  163 us (31%)
  waiting for transfers between devices  157 us (29%)
  local copies, waits for them, and re-layouts  81.4 us (15%)
  matrix products  52.1 us (10%)
  other arithmetic  48.5 us (9%)
  between operations  14.3 us (3%)
  starting transfers between devices  10.7 us (2%)
    all_gather x1, waiting for transfers between devices, per_device(): gathered = lax.all_gather(mlp_normed, 'ctx', axis=0, tiled=True)  76.2 us
    all_to_all x1, blocking collectives, side_by_side(): lax.all_to_all(both, axis, split_axis=split_dim, concat_axis=concat_dim,...  72.6 us
    all_gather x1, waiting for transfers between devices, side_by_side_2(): lax.all_gather(both, axis, axis=dim, tiled=True)  71.2 us
    all_to_all x1, blocking collectives, sent_and_summed(): lax.all_to_all(in_blocks(array, dim, count), axis, 0, 0, tiled=True)  57.5 us
    all_to_all x2, blocking collectives, sent_to_all(): lax.all_to_all(jnp.broadcast_to(array[None], (count, *array.shape)), axis...  33.2 us
    reshape x4, local copies, waits for them, and re-layouts, sinusoid(): jnp.stack([jnp.sin(angles), jnp.cos(angles)], axis=-1)  31.9 us
    sin x2, other arithmetic, sinusoid(): jnp.sin(angles)  22.2 us
    another operation x2, local copies, waits for them, and re-layouts, sinusoid(): jnp.stack([jnp.sin(angles), jnp.cos(angles)], axis=-1)  20.7 us
  transfers between devices with their start and end apart: 5, of which 3 were waited for; matrix products, arithmetic and copies ran while one was open for 20% of the time, Pallas kernels for 0%

commit v1 on v0

v1 whole, which is shorter than its diff:
```python
import math

import jax
import jax.numpy as jnp
from jax import lax
from jax.experimental import pallas as pl
from jax.experimental.pallas import tpu as pltpu
from jax.sharding import PartitionSpec as P

MESH = pl.DeviceIdType.MESH
HD = 128
D = 2048
LATENTS = 1024
EPSILON = 1e-06
MASKED = -1e30
SCALE = 1.0 / math.sqrt(HD)
BF = jnp.bfloat16
F32 = jnp.float32
VLIMIT = 56 * 1024 * 1024


def place():
    g = lax.axis_index("ctx")
    y = lax.axis_index("lat")
    return g // 16, (g // 4) % 4, (g // 2) % 2, g % 2, y


def at(x, a, b, c, y):
    return (16 * x + 4 * a + 2 * b + c, y)


def push(src, dst, send_sem, recv_sem, device):
    copy = pltpu.make_async_remote_copy(
        src_ref=src,
        dst_ref=dst,
        send_sem=send_sem,
        recv_sem=recv_sem,
        device_id=device,
        device_id_type=MESH,
    )
    return copy


def arrive(dst, recv_sem, device):
    push(dst, dst, recv_sem, recv_sem, device).wait_recv()


def greet(devices):
    barrier = pltpu.get_barrier_semaphore()
    for device in devices:
        pl.semaphore_signal(barrier, inc=1, device_id=device, device_id_type=MESH)
    pl.semaphore_wait(barrier, len(devices))


def each(first, last, body):
    def step(k, carry):
        body(k)
        return carry

    lax.fori_loop(first, last, step, 0)


class Exchange:
    def __init__(self, src, dst, send, recv, me, device_of, n, whole=False):
        self.src, self.dst, self.send, self.recv = src, dst, send, recv
        self.me, self.device_of, self.n, self.whole = me, device_of, n, whole

    def copy(self, j):
        src = self.src if self.whole else self.src.at[j]
        return push(src, self.dst.at[self.me], self.send.at[j], self.recv.at[self.me], self.device_of(j))

    def start(self):
        def one(k):
            self.copy((self.me + k) % self.n).start()

        each(1, self.n, one)
        self.dst[self.me] = self.src[...] if self.whole else self.src[self.me]

    def wait_all(self):
        def one(k):
            j = (self.me + self.n - k) % self.n
            arrive(self.dst.at[j], self.recv.at[j], self.device_of(j))

        each(1, self.n, one)

    def wait_sent(self):
        def one(k):
            self.copy((self.me + k) % self.n).wait_send()

        each(1, self.n, one)


def rms_rows(values):
    return values * lax.rsqrt(jnp.mean(values * values, axis=-1, keepdims=True) + EPSILON)


def gather_kernel(q_ref, kv_ref, tok_ref, w_ref, t_ref, stage, s1, r1, s2, r2, s3, r3):
    x, a, b, c, y = place()
    k = 2 * b + c
    j_me = 2 * x + b
    partner = at(x, a, b, 1 - c, y)
    heads = [((a + d) % 4) for d in range(1, 4)]
    rows = [((x + dx) % 4, (b + db) % 2) for dx in (0, 1, 3, 2) for db in (0, 1) if dx or db]
    greet([at(x, h, b, c, y) for h in heads] + [at(rx, a, rb, c, y) for rx, rb in rows] + [partner])
    for h in range(4):
        stage[h, 0] = q_ref[:, 128 * h : 128 * h + 128]
        stage[h, 1] = kv_ref[0, :, 128 * h : 128 * h + 128]
        stage[h, 2] = kv_ref[1, :, 128 * h : 128 * h + 128]
    first = []
    for h in heads:
        there = at(x, h, b, c, y)
        first.append(push(tok_ref, t_ref.at[x, a, k], s1.at[1, h], r1.at[1, a], there))
        first.append(push(stage.at[h], w_ref.at[:, x, a, k], s1.at[0, h], r1.at[0, a], there))
    for copy in first:
        copy.start()
    t_ref[x, a, k] = tok_ref[...]
    w_ref[0, x, a, k] = stage[a, 0]
    w_ref[1, x, a, k] = stage[a, 1]
    w_ref[2, x, a, k] = stage[a, 2]
    for h in heads:
        arrive(t_ref.at[x, h, k], r1.at[1, h], partner)
        arrive(w_ref.at[:, x, h, k], r1.at[0, h], partner)
    second = []
    for rx, rb in rows:
        there = at(rx, a, rb, c, y)
        j = 2 * rx + rb
        second.append(push(t_ref.at[x, :, k], t_ref.at[x, :, k], s2.at[1, j], r2.at[1, j_me], there))
        second.append(push(w_ref.at[:, x, :, k], w_ref.at[:, x, :, k], s2.at[0, j], r2.at[0, j_me], there))
    for copy in second:
        copy.start()

    def onward(rx, rb):
        j = 2 * rx + rb
        k2 = 2 * rb + c
        return [
            push(t_ref.at[rx, :, k2], t_ref.at[rx, :, k2], s3.at[1, j], r3.at[1, j], partner),
            push(w_ref.at[:, rx, :, k2], w_ref.at[:, rx, :, k2], s3.at[0, j], r3.at[0, j], partner),
        ]

    third = onward(x, b)
    for copy in third:
        copy.start()
    for rx, rb in rows:
        sx, sb = (2 * x + 4 - rx) % 4, rb
        j = 2 * sx + sb
        k2 = 2 * sb + c
        arrive(t_ref.at[sx, :, k2], r2.at[1, j], partner)
        arrive(w_ref.at[:, sx, :, k2], r2.at[0, j], partner)
        more = onward(sx, sb)
        for copy in more:
            copy.start()
        third += more
    for rx, rb in [(x, b)] + rows:
        j = 2 * rx + rb
        k3 = 2 * rb + 1 - c
        arrive(t_ref.at[rx, :, k3], r3.at[1, j], partner)
        arrive(w_ref.at[:, rx, :, k3], r3.at[0, j], partner)
    for copy in first + second + third:
        copy.wait_send()


def gathered(cross_q, cross_kv, token_rows):
    dma = pltpu.SemaphoreType.DMA
    return pl.pallas_call(
        gather_kernel,
        out_shape=(
            jax.ShapeDtypeStruct((3, 4, 4, 4, 32, HD), BF),
            jax.ShapeDtypeStruct((4, 4, 4, 8, 128), jnp.int32),
        ),
        in_specs=[pl.BlockSpec(memory_space=pltpu.VMEM)] * 3,
        out_specs=(pl.BlockSpec(memory_space=pltpu.VMEM),) * 2,
        scratch_shapes=[
            pltpu.VMEM((4, 3, 32, HD), BF),
            dma((2, 4)),
            dma((2, 4)),
            dma((2, 8)),
            dma((2, 8)),
            dma((2, 8)),
            dma((2, 8)),
        ],
        compiler_params=pltpu.CompilerParams(
            collective_id=0, has_side_effects=True, vmem_limit_bytes=VLIMIT
        ),
    )(cross_q, cross_kv, token_rows)


def cross_kernel(
    offset_ref, tok_ref, kpos_ref, table_ref, base_ref, mid_ref, low_ref, w_ref,
    o_ref, st_ref, lat_ref,
    wkv, rows_sin, rows_cos, looked, block, keys, values, queries,
):
    wkv[:, :HD] = w_ref[1]
    wkv[:, HD:] = w_ref[2]
    vocab = lax.broadcasted_iota(jnp.int32, (128, 256), 1)

    def embed(n):
        s, c = base_ref[0, pl.ds(n, 1)], base_ref[1, pl.ds(n, 1)]
        rows_sin[...] = s * mid_ref[1] + c * mid_ref[0]
        rows_cos[...] = c * mid_ref[1] - s * mid_ref[0]

        def quarter(part):
            at_row = pl.multiple_of(n * 512 + part * 128, 128)
            one_hot = (tok_ref[pl.ds(at_row, 128), :] == vocab).astype(BF)
            looked[...] = jnp.dot(one_hot, table_ref[...], preferred_element_type=F32)

            def sixteen(g):
                m = part * 8 + g
                row = pl.multiple_of(g * 16, 16)
                values_here = (
                    looked[pl.ds(row, 16), :]
                    + rows_sin[pl.ds(m, 1), :] * low_ref[1]
                    + rows_cos[pl.ds(m, 1), :] * low_ref[0]
                )
                out_row = pl.multiple_of(part * 128 + g * 16, 16)
                block[pl.ds(out_row, 16), :] = rms_rows(values_here).astype(BF)

            each(0, 8, sixteen)

        each(0, 4, quarter)

    def context_run(n):
        embed(n)
        both = jnp.dot(block[...], wkv[...], preferred_element_type=F32).astype(BF)
        row = pl.multiple_of(n * 512, 512)
        keys[pl.ds(row, 512), :] = both[:, :HD]
        values[pl.ds(row, 512), :] = both[:, HD:]

    each(0, 4, context_run)

    def latent_run(n):
        embed(4 + n)
        row = pl.multiple_of(n * 512, 512)
        lat_ref[pl.ds(row, 512), :] = block[...]
        queries[pl.ds(row, 512), :] = jnp.dot(block[...], w_ref[0], preferred_element_type=F32).astype(BF)

    each(0, 2, latent_run)

    def attend(t, carry):
        maxima, totals = carry
        row = pl.multiple_of(t * 256, 256)
        scores = lax.dot_general(
            queries[pl.ds(row, 256), :], keys[...], (((1,), (1,)), ((), ())), preferred_element_type=F32
        )
        scores = scores * SCALE
        qpos = offset_ref[0] + t * 256 + lax.broadcasted_iota(jnp.int32, (256, 1), 0)
        scores = jnp.where(kpos_ref[...] > qpos, MASKED, scores)
        peak = jnp.max(scores, axis=1, keepdims=True)
        weights = jnp.exp(scores - peak).astype(BF)
        total = jnp.sum(weights.astype(F32), axis=1, keepdims=True)
        out = jnp.dot(weights, values[...], preferred_element_type=F32).astype(BF)
        o_ref[:, t] = out.reshape(16, 16, HD)
        lane = lax.broadcasted_iota(jnp.int32, (16, 16, 128), 2)
        sub = lax.broadcasted_iota(jnp.int32, (16, 16, 128), 1)
        mine = lane == sub + 16 * t
        maxima = maxima + jnp.sum(jnp.where(mine, peak.reshape(16, 16, 1), 0.0), axis=1)
        totals = totals + jnp.sum(jnp.where(mine, total.reshape(16, 16, 1), 0.0), axis=1)
        return maxima, totals

    zero = jnp.zeros((16, 128), F32)
    maxima, totals = lax.fori_loop(0, 4, attend, (zero, zero))
    for r in range(16):
        st_ref[r, 0:1, :] = maxima[r : r + 1]
        st_ref[r, 1:2, :] = totals[r : r + 1]


def crossed(offset, tokens, kpos, table, base, mid, low, weights):
    vmem = pl.BlockSpec(memory_space=pltpu.VMEM)
    return pl.pallas_call(
        cross_kernel,
        out_shape=(
            jax.ShapeDtypeStruct((16, 4, 16, HD), BF),
            jax.ShapeDtypeStruct((16, 8, 128), F32),
            jax.ShapeDtypeStruct((LATENTS, D), BF),
        ),
        in_specs=[pl.BlockSpec(memory_space=pltpu.SMEM)] + [vmem] * 7,
        out_specs=(vmem,) * 3,
        scratch_shapes=[
            pltpu.VMEM((D, 2 * HD), BF),
            pltpu.VMEM((32, D), F32),
            pltpu.VMEM((32, D), F32),
            pltpu.VMEM((128, D), F32),
            pltpu.VMEM((512, D), BF),
            pltpu.VMEM((2048, HD), BF),
            pltpu.VMEM((2048, HD), BF),
            pltpu.VMEM((LATENTS, HD), BF),
        ],
        compiler_params=pltpu.CompilerParams(vmem_limit_bytes=VLIMIT),
    )(offset, tokens, kpos, table, base, mid, low, weights)


def middle_kernel(
    o_ref, st_ref, lat_ref, cout_ref, sqkv_ref, sout_ref,
    second_ref,
    ro, rst, w_co, w_qkv, w_so, msg, came, own, all_rows, normed, kv, kv_all, msg2, came2,
    load, s_o, r_o, s_st, r_st, s_m, r_m, s_a, r_a, s_kv, r_kv, s_m2, r_m2,
):
    x, a, b, c, y = place()
    r = 4 * x + 2 * b + c
    p = 4 * y + a
    row_of = lambda j: at(j // 4, a, (j // 2) % 2, j % 2, y)
    head_of = lambda j: at(x, j % 4, b, c, j // 4)
    row_at = pl.multiple_of(a * HD, HD)
    loads = [
        pltpu.make_async_copy(cout_ref.at[pl.ds(row_at, HD), :], w_co, load.at[0]),
        pltpu.make_async_copy(sqkv_ref.at[:, :, pl.ds(row_at, HD)], w_qkv, load.at[1]),
        pltpu.make_async_copy(sout_ref.at[pl.ds(row_at, HD), :], w_so, load.at[2]),
    ]
    for copy in loads:
        copy.start()
    greet([row_of((r + k) % 16) for k in range(1, 16)] + [head_of((p + k) % 16) for k in range(1, 16)])
    outs = Exchange(o_ref, ro, s_o, r_o, r, row_of, 16)
    stats = Exchange(st_ref, rst, s_st, r_st, r, row_of, 16)
    stats.start()
    outs.start()
    stats.wait_all()
    outs.wait_all()
    maxima, totals = rst[:, 0, :], rst[:, 1, :]
    factor = jnp.exp(maxima - jnp.max(maxima, axis=0, keepdims=True))
    factor = factor / jnp.sum(factor * totals, axis=0, keepdims=True)
    diagonal = lax.broadcasted_iota(jnp.int32, (64, 128), 0) == lax.broadcasted_iota(jnp.int32, (64, 128), 1)
    attended = jnp.zeros((64, HD), F32)
    for j in range(16):
        column = jnp.sum(jnp.where(diagonal, factor[j : j + 1, :], 0.0), axis=1, keepdims=True)
        attended = attended + column * ro[j].astype(F32)
    loads[0].wait()
    loads[1].wait()
    loads[2].wait()

    def shares(rows, weight, out):
        for q in range(4):
            part = jnp.dot(rows, weight[:, 512 * q : 512 * q + 512], preferred_element_type=F32).astype(BF)
            for t in range(4):
                out[4 * t + q] = part[16 * t : 16 * t + 16]

    shares(attended.astype(BF), w_co, msg)
    summed = Exchange(msg, came, s_m, r_m, p, head_of, 16)
    summed.start()
    summed.wait_all()
    first = jnp.sum(came[...].astype(F32), axis=0) + lat_ref[...].astype(F32)
    own[...] = first.astype(BF)
    spread = Exchange(own, all_rows, s_a, r_a, p, head_of, 16, whole=True)
    spread.start()
    spread.wait_all()
    for t in range(4):
        rows = jnp.concatenate([all_rows[4 * t + q] for q in range(4)], axis=1).astype(F32)
        normed[16 * t : 16 * t + 16, :] = rms_rows(rows).astype(BF)
    query = jnp.dot(normed[...], w_qkv[0], preferred_element_type=F32).astype(BF)
    kv[:, :HD] = jnp.dot(normed[...], w_qkv[1], preferred_element_type=F32).astype(BF)
    kv[:, HD:] = jnp.dot(normed[...], w_qkv[2], preferred_element_type=F32).astype(BF)
    both = Exchange(kv, kv_all, s_kv, r_kv, r, row_of, 16, whole=True)
    both.start()
    both.wait_all()
    keys = kv_all[:, :, :HD].reshape(LATENTS, HD)
    values = kv_all[:, :, HD:].reshape(LATENTS, HD)
    scores = lax.dot_general(query, keys, (((1,), (1,)), ((), ())), preferred_element_type=F32) * SCALE
    row = lax.broadcasted_iota(jnp.int32, (64, 1), 0)
    col = lax.broadcasted_iota(jnp.int32, (1, LATENTS), 1)
    row_place = (row // 16) * 256 + 16 * r + row % 16
    col_place = ((col // 16) % 4) * 256 + 16 * (col // 64) + col % 16
    scores = jnp.where(col_place > row_place, MASKED, scores)
    weights = jnp.exp(scores - jnp.max(scores, axis=1, keepdims=True)).astype(BF)
    total = jnp.sum(weights.astype(F32), axis=1, keepdims=True)
    attended = jnp.dot(weights, values, preferred_element_type=F32) / total
    shares(attended.astype(BF), w_so, msg2)
    summed2 = Exchange(msg2, came2, s_m2, r_m2, p, head_of, 16)
    summed2.start()
    summed2.wait_all()
    second_ref[...] = first + jnp.sum(came2[...].astype(F32), axis=0)
    for exchange in (outs, stats, summed, spread, both, summed2):
        exchange.wait_sent()


def middle(outs, stats, latent, cross_out, self_qkv, self_out):
    vmem = pl.BlockSpec(memory_space=pltpu.VMEM)
    hbm = pl.BlockSpec(memory_space=pl.ANY)
    dma = pltpu.SemaphoreType.DMA
    return pl.pallas_call(
        middle_kernel,
        out_shape=jax.ShapeDtypeStruct((16, 512), F32),
        in_specs=[vmem] * 3 + [hbm] * 3,
        out_specs=vmem,
        scratch_shapes=[
            pltpu.VMEM((16, 64, HD), BF),
            pltpu.VMEM((16, 8, 128), F32),
            pltpu.VMEM((HD, D), BF),
            pltpu.VMEM((3, D, HD), BF),
            pltpu.VMEM((HD, D), BF),
            pltpu.VMEM((16, 16, 512), BF),
            pltpu.VMEM((16, 16, 512), BF),
            pltpu.VMEM((16, 512), BF),
            pltpu.VMEM((16, 16, 512), BF),
            pltpu.VMEM((64, D), BF),
            pltpu.VMEM((64, 2 * HD), BF),
            pltpu.VMEM((16, 64, 2 * HD), BF),
            pltpu.VMEM((16, 16, 512), BF),
            pltpu.VMEM((16, 16, 512), BF),
            dma((3,)),
        ]
        + [dma((16,))] * 12,
        compiler_params=pltpu.CompilerParams(
            collective_id=1, has_side_effects=True, vmem_limit_bytes=VLIMIT
        ),
    )(outs, stats, latent, cross_out, self_qkv, self_out)


def mlp_kernel(
    second_ref, in_ref, mout_ref,
    out_ref,
    own, group, all_rows, normed, partial, halves, half_in, msg, came, last, came_last,
    s_h, r_h, s_r, r_r, s_p, r_p, s_x, r_x, s_m, r_m, s_l, r_l,
):
    x, a, b, c, y = place()
    r = 4 * x + 2 * b + c
    partner = at(x, a, b, 1 - c, y)
    j_me = 2 * x + b
    f = 4 * x + a
    k_me = 2 * b + c
    head_of = lambda j: at(x, j, b, c, y)
    rows = [((x + dx) % 4, (b + db) % 2) for dx in (0, 1, 3, 2) for db in (0, 1) if dx or db]
    final_of = lambda j: at(j // 4, j % 4, b, c, y)
    quad_of = lambda j: at(x, a, j // 2, j % 2, y)
    greet(
        [head_of((a + d) % 4) for d in range(1, 4)]
        + [at(rx, a, rb, c, y) for rx, rb in rows]
        + [final_of((f + k) % 16) for k in range(1, 16)]
        + [quad_of((k_me + k) % 4) for k in range(1, 4)]
    )
    own[...] = second_ref[...].astype(BF)
    heads = Exchange(own, group, s_h, r_h, a, head_of, 4, whole=True)
    heads.start()
    heads.wait_all()
    second = []
    for rx, rb in rows:
        second.append(push(group, all_rows.at[r], s_r.at[2 * rx + rb], r_r.at[j_me], at(rx, a, rb, c, y)))
    for copy in second:
        copy.start()
    all_rows[r] = group[...]
    onward = [push(group, all_rows.at[r], s_p.at[j_me], r_p.at[j_me], partner)]
    onward[0].start()
    for rx, rb in rows:
        sx, sb = (2 * x + 4 - rx) % 4, rb
        j = 2 * sx + sb
        slot = all_rows.at[4 * sx + 2 * sb + c]
        arrive(slot, r_r.at[j], partner)
        copy = push(slot, slot, s_p.at[j], r_p.at[j], partner)
        copy.start()
        onward.append(copy)
    for rx, rb in [(x, b)] + rows:
        arrive(all_rows.at[4 * rx + 2 * rb + 1 - c], r_p.at[2 * rx + rb], partner)
    def norm_one(t):
        wide = jnp.concatenate([all_rows[t, q] for q in range(4)], axis=1).astype(F32)
        normed[pl.ds(pl.multiple_of(t * 16, 16), 16), :] = rms_rows(wide).astype(BF)

    each(0, 16, norm_one)
    pre = jnp.dot(normed[...], in_ref[...], preferred_element_type=F32)
    hidden = jax.nn.gelu(pre, approximate=True).astype(BF)
    for q in range(4):
        partial[:, 512 * q : 512 * q + 512] = jnp.dot(
            hidden, mout_ref[:, 512 * q : 512 * q + 512], preferred_element_type=F32
        )
    here = (pl.ds(pl.multiple_of(r * 16, 16), 16), pl.ds(pl.multiple_of(a * 512, 512), 512))
    partial[here] = partial[here] + second_ref[...]
    other_cols = pl.ds(pl.multiple_of((1 - c) * 1024, 1024), 1024)
    own_cols = pl.ds(pl.multiple_of(c * 1024, 1024), 1024)
    halves[...] = partial[:, other_cols].astype(BF)
    swap = push(halves, half_in, s_x.at[0], r_x.at[0], partner)
    swap.start()
    swap.wait_recv()
    msg[...] = (partial[:, own_cols] + half_in[...].astype(F32)).astype(BF).reshape(16, 16, 1024)
    summed = Exchange(msg, came, s_m, r_m, f, final_of, 16)
    summed.start()
    summed.wait_all()
    last[...] = jnp.sum(came[...].astype(F32), axis=0).astype(BF)
    ends = Exchange(last, came_last, s_l, r_l, k_me, quad_of, 4, whole=True)
    ends.start()
    ends.wait_all()
    for h in range(2):
        both = came_last[h].astype(F32) + came_last[2 + h].astype(F32)
        chosen = jnp.zeros((4, 1024), F32)
        for k in range(4):
            chosen = chosen + jnp.where(k_me == k, both[4 * k : 4 * k + 4], 0.0)
        out_ref[:, 1024 * h : 1024 * h + 1024] = chosen
    for copy in second + onward + [swap]:
        copy.wait_send()
    for exchange in (heads, summed, ends):
        exchange.wait_sent()


def fed_forward(second, mlp_in, mlp_out):
    vmem = pl.BlockSpec(memory_space=pltpu.VMEM)
    dma = pltpu.SemaphoreType.DMA
    return pl.pallas_call(
        mlp_kernel,
        out_shape=jax.ShapeDtypeStruct((4, D), F32),
        in_specs=[vmem] * 3,
        out_specs=vmem,
        scratch_shapes=[
            pltpu.VMEM((16, 512), BF),
            pltpu.VMEM((4, 16, 512), BF),
            pltpu.VMEM((16, 4, 16, 512), BF),
            pltpu.VMEM((256, D), BF),
            pltpu.VMEM((256, D), F32),
            pltpu.VMEM((256, 1024), BF),
            pltpu.VMEM((256, 1024), BF),
            pltpu.VMEM((16, 16, 1024), BF),
            pltpu.VMEM((16, 16, 1024), BF),
            pltpu.VMEM((16, 1024), BF),
            pltpu.VMEM((4, 16, 1024), BF),
            dma((4,)),
            dma((4,)),
            dma((8,)),
            dma((8,)),
            dma((8,)),
            dma((8,)),
            dma((1,)),
            dma((1,)),
            dma((16,)),
            dma((16,)),
            dma((4,)),
            dma((4,)),
        ],
        compiler_params=pltpu.CompilerParams(
            collective_id=2, has_side_effects=True, vmem_limit_bytes=VLIMIT
        ),
    )(second, mlp_in, mlp_out)


def per_device(
    token_ids,
    latent_offset,
    embed_table,
    cross_q,
    cross_kv,
    cross_out,
    self_qkv,
    self_out,
    mlp_in,
    mlp_out,
):
    x, a, b, c, y = place()
    r = 4 * x + 2 * b + c
    offset = latent_offset[0]
    feature = jnp.arange(D, dtype=jnp.int32)
    rates = jnp.exp((feature // 2).astype(F32) * (-2.0 * math.log(10000.0) / D))
    block_starts = 512 * (16 * x + 4 * jnp.arange(4, dtype=jnp.int32) + 2 * b + c)
    starts = jnp.concatenate([block_starts, jnp.stack([offset, offset + 512, offset, offset])])
    places = jnp.concatenate([starts, 16 * jnp.arange(32, dtype=jnp.int32), jnp.arange(16, dtype=jnp.int32)])
    angles = places.astype(F32)[:, None] * rates[None, :]
    sines, cosines = jnp.sin(angles), jnp.cos(angles)
    odd = (feature % 2 == 1)[None, :]
    base = jnp.stack([jnp.where(odd, cosines[:8], sines[:8]), jnp.where(odd, -sines[:8], cosines[:8])])
    mid = jnp.stack([sines[8:40], cosines[8:40]])
    low = jnp.stack([sines[40:], cosines[40:]])

    token_rows = jnp.pad(token_ids.reshape(4, 128), ((0, 4), (0, 0)))
    weights, tokens = gathered(cross_q, cross_kv, token_rows)
    tokens = tokens[:, :, :, :4].reshape(64, 512)
    mine = lax.dynamic_index_in_dim(tokens.reshape(4, 4, 4, 512), x, 0, keepdims=False)
    mine = lax.dynamic_index_in_dim(mine, 2 * b + c, 1, keepdims=False).reshape(2048)
    latent_tokens = lax.dynamic_slice_in_dim(tokens.reshape(-1), offset, LATENTS, 0)
    column = jnp.concatenate([mine, latent_tokens])[:, None]
    kpos = (block_starts[:, None] + jnp.arange(512, dtype=jnp.int32)[None, :]).reshape(1, 2048)
    outs, stats, latent = crossed(
        latent_offset, column, kpos, embed_table, base, mid, low, weights.reshape(3, D, HD)
    )
    own_latent = lax.dynamic_slice(latent, (y * 256 + r * 16, a * 512), (16, 512))
    second = middle(outs.reshape(16, 64, HD), stats, own_latent, cross_out, self_qkv, self_out)
    return fed_forward(second, mlp_in, mlp_out).astype(BF)[None]


def solution(mesh):
    placed = (
        P("ctx"),
        P(),
        P(),
        P("ctx", "lat"),
        P(None, "ctx", "lat"),
        P("lat", None),
        P(None, None, "lat"),
        P("lat", None),
        P(None, "ctx"),
        P("ctx", None),
    )
    return jax.shard_map(
        per_device, mesh=mesh, in_specs=placed, out_specs=P("lat", "ctx", None), check_vma=False
    )
```

time: 533 us -> 185 us (0.35)
  Pallas kernels: 0 us -> 172 us
  blocking collectives: 163 us -> 0 us
  waiting for transfers between devices: 157 us -> 0 us
  local copies, waits for them, and re-layouts: 81.4 us -> 6.2 us
  matrix products: 52.1 us -> 0 us
  other arithmetic: 48.5 us -> 5.33 us
  between operations: 14.3 us -> 0.76 us
  starting transfers between devices: 10.7 us -> 0 us
    pallas_call x0 -> x4, Pallas kernels: none -> 172 us  [the longest x1 50.8 us: middle(): pl.pallas_call(middle_kernel, out_shape=jax.ShapeDtypeStruct((16, 512), F...]
    all_to_all x4 -> x0, blocking collectives: 163 us -> none  [the longest x1 72.6 us: side_by_side(): lax.all_to_all(both, axis, split_axis=split_dim, concat_axis=concat_dim,...]
    all_gather x3 -> x0, waiting for transfers between devices: 147 us -> none  [the longest x1 76.2 us: per_device(): gathered = lax.all_gather(mlp_normed, 'ctx', axis=0, tiled=True)]
    dot_general x27 -> x0, matrix products: 52.1 us -> none  [the longest x8 10.6 us: one_head(): lax.dot_general(query, key, (((1,), (1,)), ((), ())), preferred_element_t...]
    reshape x11 -> x0, local copies, waits for them, and re-layouts: 39 us -> none  [the longest x4 31.9 us: sinusoid(): jnp.stack([jnp.sin(angles), jnp.cos(angles)], axis=-1)]
    sin x2 -> x0, other arithmetic: 22.2 us -> none  [sinusoid(): jnp.sin(angles)]
    another operation x2 -> x3, local copies, waits for them, and re-layouts: 20.7 us -> 0.13 us  [the longest x1 0.08 us: per_device(): tokens.reshape(4, 4, 4, 512)]
    reduce_sum x15 -> x0, other arithmetic: 10.9 us -> none  [the longest x8 3.13 us: one_head(): total = jnp.sum(weights.astype(jnp.float32), axis=1)]
  transfers between devices with their start and end apart: 5 -> 0, of which waited for: 3 -> 0; matrix products, arithmetic and copies ran while one was open for 20% -> 0% of each run, Pallas kernels for 0% -> 0%
where the time goes in v1:
time: 185 us; the launch traced here: 184 us
  Pallas kernels  172 us (93%)
  local copies, waits for them, and re-layouts  6.2 us (3%)
  other arithmetic  5.33 us (3%)
    pallas_call x1, Pallas kernels, middle(): pl.pallas_call(middle_kernel, out_shape=jax.ShapeDtypeStruct((16, 512), F...  50.8 us
    pallas_call x1, Pallas kernels, crossed(): pl.pallas_call(cross_kernel, out_shape=(jax.ShapeDtypeStruct((16, 4, 16,...  48.3 us
    pallas_call x1, Pallas kernels, fed_forward(): pl.pallas_call(mlp_kernel, out_shape=jax.ShapeDtypeStruct((4, D), F32), i...  42.8 us
    pallas_call x1, Pallas kernels, gathered(): pl.pallas_call(gather_kernel, out_shape=(jax.ShapeDtypeStruct((3, 4, 4, 4...  29.9 us

profile of v1, /device:TPU:1, one launch (start us, length us, event | category | flops | bytes accessed | tf_op | source)
XLA Modules:
  0.0 184.1 jit_solution(1944126218042923765)
XLA Ops:
  0.7 0.1 concatenate.14
  0.8 1.3 pad.4.tok_ref
  2.1 0.1 add_bitcast_fusion
  2.1 0.6 copy.12
  2.8 1.7 multiply_cosine_fusion
  4.5 0.6 pad_maximum_fusion.2.base_ref
  5.2 0.8 pad_maximum_fusion.mid_ref
  6.0 0.7 pad_maximum_fusion.1.low_ref
  6.7 29.9 %shard_map.100 = (bf16[3,4,4,4,32,128]{5,4,3,2,1,0:T(8,128)(2,1)}, s32[4,4,4,8,128]{4,3,2,1,0:T(8,128)}) custom-call(bf16[32,512]{1,0:T(8,128)(2,1)} %q_ref.1, bf16[2,32,512]{2,1,0:T(8,128)(2,1)} %kv_ref.1, s32[8,128]{1,0:T(8,128)} %pad.4.tok_ref), custom_call_target="tpu_custom_call" | custom-call | tf_op jit(solution)/shard_map/pallas_call | solution.py:164
  36.6 1.0 slice.23
  37.6 0.1 dynamic_slice.13
  37.7 0.1 reshape_reshape.6
  37.8 1.7 copy.11.tok_ref
  39.5 48.3 %shard_map.101 = (bf16[16,4,16,128]{3,2,1,0:T(8,128)(2,1)}, f32[16,8,128]{2,1,0:T(8,128)}, bf16[1024,2048]{1,0:T(8,128)(2,1)}) custom-call(s32[1]{0:T(128)} %copy.13.offset_ref, s32[3072,1]{1,0:T(8,128)} %copy.11.tok_ref, s32[1,2048]{1,0:T(1,128)} %bitcast.34, bf16[256,2048]{1,0:T(8,128)(2,1)} %table_ref.1, f32[2,8,2048]{2,1,0:T(8,128)} %pad_maximum_fusion.2.base_ref, ...), custom_call_target="tpu_custom_call" | custom-call | tf_op jit(solution)/shard_map/pallas_call | solution.py:268
  87.8 1.3 dynamic_slice.14.lat_ref
  89.1 50.8 %shard_map.102.second_ref = f32[16,512]{1,0:T(8,128)} custom-call(bf16[16,64,128]{2,1,0:T(8,128)(2,1)} %bitcast.32, f32[16,8,128]{2,1,0:T(8,128)} %get-tuple-element.13.st_ref, bf16[16,512]{1,0:T(8,128)(2,1)} %dynamic_slice.14.lat_ref, bf16[512,2048]{1,0:T(8,128)(2,1)} %cout_ref.1, bf16[3,2048,512]{2,1,0:T(8,128)(2,1)} %sqkv_ref.1, bf16[512,2048]{1,0:T(8,128)(2,1)} %sout_ref.1), custom_call_target="tpu_custom_call" | custom-call | tf_op jit(solution)/shard_map/pallas_call | solution.py:377
  139.9 42.8 %shard_map.103 = f32[4,2048]{1,0:T(4,128)} custom-call(f32[16,512]{1,0:T(8,128)} %shard_map.102.second_ref, bf16[2048,128]{1,0:T(8,128)(2,1)} %in_ref.1, bf16[128,2048]{1,0:T(8,128)(2,1)} %mout_ref.1), custom_call_target="tpu_custom_call" | custom-call | tf_op jit(solution)/shard_map/pallas_call | solution.py:492
  182.7 1.4 convert_bitcast_fusion
  (11 shorter events, 0.1 us)

commit v2 on v0

v2 whole, which is shorter than its diff:
```python
import math

import jax
import jax.numpy as jnp
from jax import lax
from jax.experimental import pallas as pl
from jax.experimental.pallas import tpu as pltpu
from jax.sharding import PartitionSpec as P

MESH = pl.DeviceIdType.MESH
HD = 128
D = 2048
LATENTS = 1024
EPSILON = 1e-06
MASKED = -1e30
SCALE = 1.0 / math.sqrt(HD)
BF = jnp.bfloat16
F32 = jnp.float32
VLIMIT = 58 * 1024 * 1024


def place():
    g = lax.axis_index("ctx")
    y = lax.axis_index("lat")
    return g // 16, (g // 4) % 4, (g // 2) % 2, g % 2, y


def at(x, a, b, c, y):
    return (16 * x + 4 * a + 2 * b + c, y)


def push(src, dst, send_sem, recv_sem, device):
    copy = pltpu.make_async_remote_copy(
        src_ref=src,
        dst_ref=dst,
        send_sem=send_sem,
        recv_sem=recv_sem,
        device_id=device,
        device_id_type=MESH,
    )
    return copy


def arrive(dst, recv_sem, device):
    push(dst, dst, recv_sem, recv_sem, device).wait_recv()


def each(first, last, body):
    def step(k, carry):
        body(k)
        return carry

    lax.fori_loop(first, last, step, 0)


class Exchange:
    def __init__(self, src, dst, send, recv, me, device_of, n, whole=False):
        self.src, self.dst, self.send, self.recv = src, dst, send, recv
        self.me, self.device_of, self.n, self.whole = me, device_of, n, whole

    def copy(self, j):
        src = self.src if self.whole else self.src.at[j]
        return push(src, self.dst.at[self.me], self.send.at[j], self.recv.at[self.me], self.device_of(j))

    def start(self):
        def one(k):
            self.copy((self.me + k) % self.n).start()

        each(1, self.n, one)
        self.dst[self.me] = self.src[...] if self.whole else self.src[self.me]

    def wait_all(self):
        def one(k):
            j = (self.me + self.n - k) % self.n
            arrive(self.dst.at[j], self.recv.at[j], self.device_of(j))

        each(1, self.n, one)

    def wait_sent(self):
        def one(k):
            self.copy((self.me + k) % self.n).wait_send()

        each(1, self.n, one)


def rms_rows(values):
    return values * lax.rsqrt(jnp.mean(values * values, axis=-1, keepdims=True) + EPSILON)


def whole_kernel(
    offset_ref, sin_ref, cos_ref, tok_ref, table_ref, q_ref, kv_ref,
    cout_ref, sqkv_ref, sout_ref, in_ref, mout_ref,
    out_ref,
    stage, w_all, tokens, wkv, tw, rows_sin, rows_cos, waves, one_hot, inverse, latent, keys, values, q_own, q_all,
    o_msg, o_came, st_msg, st_came, w_co, w_qkv, w_so, msg, came, own, all_rows, normed, kv, kv_all, msg2, came2,
    own2, all_rows2, w_in, w_out, partial, msg3, came3,
    load, s1, r1, s2, r2, s3, r3, s_q, r_q, s_o, r_o, s_st, r_st, s_m, r_m, s_a, r_a, s_kv, r_kv, s_m2, r_m2,
    s_a2, r_a2, s_m3, r_m3, own_w, sw1, rw1, sw2, rw2, sw3, rw3,
):
    x, a, b, c, y = place()
    k = 2 * b + c
    r = 4 * x + k
    p = 4 * y + a
    j_me = 2 * x + b
    partner = at(x, a, b, 1 - c, y)

    def row_of(j):
        return at(j // 4, a, (j // 2) % 2, j % 2, y)

    def head_of(j):
        return at(x, j % 4, b, c, j // 4)

    def final_of(j):
        return at(x, k, (j // 2) % 2, j % 2, j // 4)

    def sender_of(j):
        return at(x, j % 4, a // 2, a % 2, j // 4)

    final_self = jnp.where(a == k, 4 * y + k, 16)
    sender_self = jnp.where(a == k, p, 16)

    row_at = pl.multiple_of(a * HD, HD)
    loads = [
        pltpu.make_async_copy(cout_ref.at[pl.ds(row_at, HD), :], w_co, load.at[0]),
        pltpu.make_async_copy(sqkv_ref.at[:, :, pl.ds(row_at, HD)], w_qkv, load.at[1]),
        pltpu.make_async_copy(sout_ref.at[pl.ds(row_at, HD), :], w_so, load.at[2]),
    ]
    for copy in loads:
        copy.start()
    barrier = pltpu.get_barrier_semaphore()

    def hello(device):
        pl.semaphore_signal(barrier, inc=1, device_id=device, device_id_type=MESH)

    each(1, 16, lambda i: hello(row_of((r + i) % 16)))
    each(1, 16, lambda i: hello(head_of((p + i) % 16)))

    def hello_sender(j):
        @pl.when(j != sender_self)
        def _():
            hello(sender_of(j))

    each(0, 16, hello_sender)
    for h in range(4):
        stage[h, 0] = q_ref[:, 128 * h : 128 * h + 128]
        stage[h, 1] = kv_ref[0, :, 128 * h : 128 * h + 128]
        stage[h, 2] = kv_ref[1, :, 128 * h : 128 * h + 128]
    pl.semaphore_wait(barrier, jnp.where(a == k, 45, 46))

    heads = [(a + d) % 4 for d in range(1, 4)]
    rows = [((x + dx) % 4, (b + db) % 2) for dx in (0, 1, 3, 2) for db in (0, 1) if dx or db]
    first_copies = []
    for h in heads:
        there = at(x, h, b, c, y)
        first_copies.append(push(tok_ref, tokens.at[x, a, k], s1.at[1, h], r1.at[1, a], there))
        first_copies.append(push(stage.at[h], w_all.at[:, x, a, k], s1.at[0, h], r1.at[0, a], there))
    for copy in first_copies:
        copy.start()
    tokens[x, a, k] = tok_ref[...]
    for part in range(3):
        w_all[part, x, a, k] = stage[a, part]

    odd = lax.broadcasted_iota(jnp.int32, (1, D), 1) % 2 == 1
    mid_sin, mid_cos = sin_ref[8:40], cos_ref[8:40]

    def start_of(n):
        s, co = sin_ref[pl.ds(n, 1)], cos_ref[pl.ds(n, 1)]
        return jnp.where(odd, co, s), jnp.where(odd, -s, co)

    def waves_of(n):
        s, co = start_of(n)
        rows_sin[...] = s * mid_cos + co * mid_sin
        rows_cos[...] = co * mid_cos - s * mid_sin

        def columns(j):
            lanes = pl.ds(pl.multiple_of(j * 128, 128), 128)
            low_sin, low_cos = sin_ref[40:56, lanes], cos_ref[40:56, lanes]
            for m in range(32):
                wave = rows_sin[m : m + 1, lanes] * low_cos + rows_cos[m : m + 1, lanes] * low_sin
                waves[pl.ds(pl.multiple_of(n * 512 + 16 * m, 16), 16), lanes] = wave.astype(BF)

        each(0, 16, columns)

    each(0, 4, waves_of)

    for h in heads:
        arrive(tokens.at[x, h, k], r1.at[1, h], partner)
        arrive(w_all.at[:, x, h, k], r1.at[0, h], partner)
    second_copies = []
    for rx, rb in rows:
        there = at(rx, a, rb, c, y)
        j = 2 * rx + rb
        second_copies.append(push(tokens.at[x, :, k], tokens.at[x, :, k], s2.at[1, j], r2.at[1, j_me], there))
        second_copies.append(push(w_all.at[:, x, :, k], w_all.at[:, x, :, k], s2.at[0, j], r2.at[0, j_me], there))
    for copy in second_copies:
        copy.start()

    def onward(rx, rb):
        j = 2 * rx + rb
        k2 = 2 * rb + c
        return [
            push(tokens.at[rx, :, k2], tokens.at[rx, :, k2], s3.at[1, j], r3.at[1, j], partner),
            push(w_all.at[:, rx, :, k2], w_all.at[:, rx, :, k2], s3.at[0, j], r3.at[0, j], partner),
        ]

    third_copies = onward(x, b)
    for copy in third_copies:
        copy.start()

    square = table_ref[...].astype(F32)
    square = square * square
    high = square.astype(BF)
    lower = (square - high.astype(F32)).astype(BF)
    ones = jnp.ones((8, D), BF)
    across = (((1,), (1,)), ((), ()))
    norms = lax.dot_general(ones, high, across, preferred_element_type=F32) + lax.dot_general(
        ones, lower, across, preferred_element_type=F32
    )
    norms = norms[0:1]
    vocab = lax.broadcasted_iota(jnp.int32, (128, 256), 1).astype(F32)
    diagonal = lax.broadcasted_iota(jnp.int32, (128, 128), 0) == lax.broadcasted_iota(jnp.int32, (128, 128), 1)

    def scales_of(n):
        here = tokens[x, n, k].astype(F32)
        row = pl.multiple_of(n * 512, 512)
        products = lax.dot_general(waves[pl.ds(row, 512), :], table_ref[...], across, preferred_element_type=F32)
        for q in range(4):
            column = jnp.sum(jnp.where(diagonal, here[q : q + 1, :], 0.0), axis=1, keepdims=True)
            chosen = column == vocab
            quarter = pl.ds(pl.multiple_of(n * 512 + 128 * q, 128), 128)
            one_hot[quarter, :] = chosen.astype(BF)
            total = jnp.sum(
                jnp.where(chosen, 2.0 * products[128 * q : 128 * q + 128] + norms, 0.0), axis=1, keepdims=True
            )
            total = jnp.maximum(total + D / 2, 0.0)
            inverse[quarter, :] = lax.rsqrt(total * (1.0 / D) + EPSILON)

    each(0, 4, scales_of)

    for rx, rb in rows:
        sx, sb = (2 * x + 4 - rx) % 4, rb
        j = 2 * sx + sb
        k2 = 2 * sb + c
        arrive(tokens.at[sx, :, k2], r2.at[1, j], partner)
        arrive(w_all.at[:, sx, :, k2], r2.at[0, j], partner)
        more = onward(sx, sb)
        for copy in more:
            copy.start()
        third_copies += more
    for rx, rb in [(x, b)] + rows:
        j = 2 * rx + rb
        k3 = 2 * rb + 1 - c
        arrive(tokens.at[rx, :, k3], r3.at[1, j], partner)
        arrive(w_all.at[:, rx, :, k3], r3.at[0, j], partner)

    main = c == y // 2
    source = jnp.logical_and(main, b == y % 2)
    beside = at(x, a, 1 - b, c, y)
    mine = [
        pltpu.make_async_copy(in_ref, w_in.at[x], own_w.at[0]),
        pltpu.make_async_copy(mout_ref, w_out.at[x], own_w.at[1]),
    ]
    step1 = [
        push(in_ref, w_in.at[x], sw1.at[0], rw1.at[0], beside),
        push(mout_ref, w_out.at[x], sw1.at[1], rw1.at[1], beside),
    ]

    @pl.when(source)
    def _():
        for copy in step1 + mine:
            copy.start()

    offset = offset_ref[0]
    slot = lax.broadcasted_iota(jnp.int32, (64, 1), 0)
    target = offset + (slot // 16) * 256 + 16 * r + slot % 16
    lane = lax.broadcasted_iota(jnp.int32, (1, 128), 1)
    found = jnp.zeros((64, 128), F32)
    for q in range(3):
        bytes_here = tokens[3, 3, 1 + q].astype(F32)
        for t in range(4):
            hit = target == lane + (31232 + 512 * q + 128 * t)
            found = found + jnp.where(hit, bytes_here[t : t + 1, :], 0.0)
    column = jnp.sum(found, axis=1, keepdims=True)
    looked = jnp.dot((column == vocab[:64]).astype(BF), table_ref[...], preferred_element_type=F32)
    for t in range(4):
        s, co = start_of(4 + t)
        wave = s * cos_ref[40:56] + co * sin_ref[40:56]
        latent[16 * t : 16 * t + 16, :] = rms_rows(looked[16 * t : 16 * t + 16] + wave).astype(BF)
    weights_of = w_all.reshape(3, D, HD)
    q_own[...] = jnp.dot(latent[...], weights_of[0], preferred_element_type=F32).astype(BF)
    asked = Exchange(q_own, q_all, s_q, r_q, r, row_of, 16, whole=True)
    asked.start()

    wkv[:, :HD] = weights_of[1]
    wkv[:, HD:] = weights_of[2]
    table_w = jnp.dot(table_ref[...], wkv[...], preferred_element_type=F32)
    tw[0] = table_w.astype(BF)
    tw[1] = (table_w - table_w.astype(BF).astype(F32)).astype(BF)

    def keys_of(n):
        run = pl.ds(pl.multiple_of(n * 512, 512), 512)
        both = jnp.dot(waves[run, :], wkv[...], preferred_element_type=F32)
        both = both + jnp.dot(one_hot[run, :], tw[0], preferred_element_type=F32)
        both = both + jnp.dot(one_hot[run, :], tw[1], preferred_element_type=F32)
        both = (both * inverse[run, :]).astype(BF)
        keys[run, :] = both[:, :HD]
        values[run, :] = both[:, HD:]

    each(0, 4, keys_of)
    asked.wait_all()

    key_col = lax.broadcasted_iota(jnp.int32, (1, 2048), 1)
    key_place = 512 * (16 * x + 4 * (key_col // 512) + k) + key_col % 512
    outs = Exchange(o_msg, o_came, s_o, r_o, r, row_of, 16)
    stats = Exchange(st_msg, st_came, s_st, r_st, r, row_of, 16)
    diagonal64 = lax.broadcasted_iota(jnp.int32, (64, 128), 0) == lax.broadcasted_iota(jnp.int32, (64, 128), 1)

    def attend(step):
        t = (x + 1 + step) % 4
        query = q_all[pl.ds(4 * t, 4)].reshape(256, HD)
        scores = lax.dot_general(query, keys[...], across, preferred_element_type=F32) * SCALE
        row = lax.broadcasted_iota(jnp.int32, (256, 1), 0)
        row_place = offset + ((row // 16) % 4) * 256 + 16 * (4 * t + row // 64) + row % 16
        scores = jnp.where(key_place > row_place, MASKED, scores)
        peak = jnp.max(scores, axis=1, keepdims=True)
        weights = jnp.exp(scores - peak).astype(BF)
        total = jnp.sum(weights.astype(F32), axis=1, keepdims=True)
        out = jnp.dot(weights, values[...], preferred_element_type=F32).astype(BF)
        for g in range(4):
            some = slice(64 * g, 64 * g + 64)
            j = 4 * t + g
            o_msg[j] = out[some]
            st_msg[j, 0:1, :] = jnp.sum(jnp.where(diagonal64, peak[some], 0.0), axis=0, keepdims=True)
            st_msg[j, 1:2, :] = jnp.sum(jnp.where(diagonal64, total[some], 0.0), axis=0, keepdims=True)

            @pl.when(j != r)
            def _():
                stats.copy(j).start()
                outs.copy(j).start()

    each(0, 4, attend)
    o_came[r] = o_msg[r]
    st_came[r] = st_msg[r]
    stats.wait_all()
    outs.wait_all()

    def forward(i):
        return [
            push(w_in.at[i], w_in.at[i], sw3.at[0, i], rw3.at[0, i], partner),
            push(w_out.at[i], w_out.at[i], sw3.at[1, i], rw3.at[1, i], partner),
        ]

    step2 = []
    for d in (1, 3, 2):
        there = at((x + d) % 4, a, b, c, y)
        step2.append(push(w_in.at[x], w_in.at[x], sw2.at[0, d], rw2.at[0, x], there))
        step2.append(push(w_out.at[x], w_out.at[x], sw2.at[1, d], rw2.at[1, x], there))

    @pl.when(source)
    def _():
        for copy in mine:
            copy.wait()

    @pl.when(jnp.logical_and(main, jnp.logical_not(source)))
    def _():
        arrive(w_in.at[x], rw1.at[0], partner)
        arrive(w_out.at[x], rw1.at[1], partner)

    @pl.when(main)
    def _():
        for copy in step2 + forward(x):
            copy.start()

    maxima, totals = st_came[:, 0, :], st_came[:, 1, :]
    factor = jnp.exp(maxima - jnp.max(maxima, axis=0, keepdims=True))
    factor = factor / jnp.sum(factor * totals, axis=0, keepdims=True)
    attended = jnp.zeros((64, HD), F32)
    for j in range(16):
        column = jnp.sum(jnp.where(diagonal64, factor[j : j + 1, :], 0.0), axis=1, keepdims=True)
        attended = attended + column * o_came[j].astype(F32)
    for copy in loads:
        copy.wait()

    def shares(rows, weight, out):
        for q in range(4):
            part = jnp.dot(rows, weight[:, 512 * q : 512 * q + 512], preferred_element_type=F32).astype(BF)
            for t in range(4):
                out[4 * t + q] = part[16 * t : 16 * t + 16]

    def rows_normed(blocks):
        for t in range(4):
            wide = jnp.concatenate([blocks[4 * t + q] for q in range(4)], axis=1).astype(F32)
            normed[16 * t : 16 * t + 16, :] = rms_rows(wide).astype(BF)

    shares(attended.astype(BF), w_co, msg)
    summed = Exchange(msg, came, s_m, r_m, p, head_of, 16)
    summed.start()
    own_block = (pl.ds(pl.multiple_of(16 * y, 16), 16), pl.ds(pl.multiple_of(512 * a, 512), 512))
    own_latent = latent[own_block].astype(F32)
    summed.wait_all()
    first = jnp.sum(came[...].astype(F32), axis=0) + own_latent
    own[...] = first.astype(BF)
    spread = Exchange(own, all_rows, s_a, r_a, p, head_of, 16, whole=True)
    spread.start()
    spread.wait_all()

    rows_normed(all_rows)
    kv[:, :HD] = jnp.dot(normed[...], w_qkv[1], preferred_element_type=F32).astype(BF)
    kv[:, HD:] = jnp.dot(normed[...], w_qkv[2], preferred_element_type=F32).astype(BF)
    both = Exchange(kv, kv_all, s_kv, r_kv, r, row_of, 16, whole=True)
    both.start()
    query = jnp.dot(normed[...], w_qkv[0], preferred_element_type=F32).astype(BF)
    both.wait_all()

    @pl.when(main)
    def _():
        for d in (1, 3, 2):
            i = (x + d) % 4
            arrive(w_in.at[i], rw2.at[0, i], partner)
            arrive(w_out.at[i], rw2.at[1, i], partner)
            for copy in forward(i):
                copy.start()

    all_keys = kv_all[:, :, :HD].reshape(LATENTS, HD)
    all_values = kv_all[:, :, HD:].reshape(LATENTS, HD)
    scores = lax.dot_general(query, all_keys, across, preferred_element_type=F32) * SCALE
    row = lax.broadcasted_iota(jnp.int32, (64, 1), 0)
    col = lax.broadcasted_iota(jnp.int32, (1, LATENTS), 1)
    row_place = (row // 16) * 256 + 16 * r + row % 16
    col_place = ((col // 16) % 4) * 256 + 16 * (col // 64) + col % 16
    scores = jnp.where(col_place > row_place, MASKED, scores)
    weights = jnp.exp(scores - jnp.max(scores, axis=1, keepdims=True)).astype(BF)
    total = jnp.sum(weights.astype(F32), axis=1, keepdims=True)
    attended = jnp.dot(weights, all_values, preferred_element_type=F32) / total
    shares(attended.astype(BF), w_so, msg2)
    summed2 = Exchange(msg2, came2, s_m2, r_m2, p, head_of, 16)
    summed2.start()
    summed2.wait_all()
    second = first + jnp.sum(came2[...].astype(F32), axis=0)
    own2[...] = second.astype(BF)
    spread2 = Exchange(own2, all_rows2, s_a2, r_a2, p, head_of, 16, whole=True)
    spread2.start()

    @pl.when(jnp.logical_not(main))
    def _():
        for i in range(4):
            arrive(w_in.at[i], rw3.at[0, i], partner)
            arrive(w_out.at[i], rw3.at[1, i], partner)

    spread2.wait_all()

    rows_normed(all_rows2)
    hidden = []
    for i in range(4):
        pre = jnp.dot(normed[...], w_in[i], preferred_element_type=F32)
        hidden.append(jax.nn.gelu(pre, approximate=True).astype(BF))
    hidden = jnp.concatenate(hidden, axis=1)
    for q in range(4):
        columns = slice(512 * q, 512 * q + 512)
        partial[q] = jnp.dot(hidden, w_out[:, :, columns].reshape(512, 512), preferred_element_type=F32)
    here = pl.ds(pl.multiple_of(16 * y, 16), 16)
    partial[a, here, :] = partial[a, here, :] + second
    for j in range(16):
        some = slice(4 * j, 4 * j + 4)
        msg3[j] = jnp.concatenate([partial[q, some, :] for q in range(4)], axis=0).astype(BF)

    def last_copy(j):
        return push(msg3.at[j], came3.at[p], s_m3.at[j], r_m3.at[p], final_of(j))

    def last_start(i):
        j = (p + i) % 16

        @pl.when(j != final_self)
        def _():
            last_copy(j).start()

    each(0, 16, last_start)

    @pl.when(a == k)
    def _():
        came3[p] = msg3[4 * y + k]

    def last_wait(i):
        j = (p + i) % 16

        @pl.when(j != sender_self)
        def _():
            arrive(came3.at[j], r_m3.at[j], partner)

    each(0, 16, last_wait)
    ended = jnp.sum(came3[...].astype(F32), axis=0)
    for q in range(4):
        out_ref[:, 512 * q : 512 * q + 512] = ended[4 * q : 4 * q + 4]

    for copy in first_copies + second_copies + third_copies:
        copy.wait_send()
    for exchange in (asked, outs, stats, summed, spread, both, summed2, spread2):
        exchange.wait_sent()

    def last_sent(i):
        j = (p + i) % 16

        @pl.when(j != final_self)
        def _():
            last_copy(j).wait_send()

    each(0, 16, last_sent)

    @pl.when(source)
    def _():
        for copy in step1:
            copy.wait_send()

    @pl.when(main)
    def _():
        for copy in step2:
            copy.wait_send()
        for i in range(4):
            for copy in forward(i):
                copy.wait_send()


def per_device(
    token_ids,
    latent_offset,
    embed_table,
    cross_q,
    cross_kv,
    cross_out,
    self_qkv,
    self_out,
    mlp_in,
    mlp_out,
):
    x, a, b, c, y = place()
    r = 4 * x + 2 * b + c
    feature = jnp.arange(D, dtype=jnp.int32)
    rates = jnp.exp((feature // 2).astype(F32) * (-2.0 * math.log(10000.0) / D))
    four = jnp.arange(4, dtype=jnp.int32)
    places = jnp.concatenate(
        [
            512 * (16 * x + 4 * four + 2 * b + c),
            latent_offset[0] + 256 * four + 16 * r,
            16 * jnp.arange(32, dtype=jnp.int32),
            jnp.arange(16, dtype=jnp.int32),
        ]
    )
    angles = places.astype(F32)[:, None] * rates[None, :]
    vmem = pl.BlockSpec(memory_space=pltpu.VMEM)
    hbm = pl.BlockSpec(memory_space=pl.ANY)
    dma = pltpu.SemaphoreType.DMA
    rows = pl.pallas_call(
        whole_kernel,
        out_shape=jax.ShapeDtypeStruct((4, D), F32),
        in_specs=[pl.BlockSpec(memory_space=pltpu.SMEM)] + [vmem] * 6 + [hbm] * 5,
        out_specs=vmem,
        scratch_shapes=[
            pltpu.VMEM((4, 3, 32, HD), BF),
            pltpu.VMEM((3, 4, 4, 4, 32, HD), BF),
            pltpu.VMEM((4, 4, 4, 4, 128), jnp.int32),
            pltpu.VMEM((D, 2 * HD), BF),
            pltpu.VMEM((2, 256, 2 * HD), BF),
            pltpu.VMEM((32, D), F32),
            pltpu.VMEM((32, D), F32),
            pltpu.VMEM((2048, D), BF),
            pltpu.VMEM((2048, 256), BF),
            pltpu.VMEM((2048, 1), F32),
            pltpu.VMEM((64, D), BF),
            pltpu.VMEM((2048, HD), BF),
            pltpu.VMEM((2048, HD), BF),
            pltpu.VMEM((64, HD), BF),
            pltpu.VMEM((16, 64, HD), BF),
            pltpu.VMEM((16, 64, HD), BF),
            pltpu.VMEM((16, 64, HD), BF),
            pltpu.VMEM((16, 8, 128), F32),
            pltpu.VMEM((16, 8, 128), F32),
            pltpu.VMEM((HD, D), BF),
            pltpu.VMEM((3, D, HD), BF),
            pltpu.VMEM((HD, D), BF),
            pltpu.VMEM((16, 16, 512), BF),
            pltpu.VMEM((16, 16, 512), BF),
            pltpu.VMEM((16, 512), BF),
            pltpu.VMEM((16, 16, 512), BF),
            pltpu.VMEM((64, D), BF),
            pltpu.VMEM((64, 2 * HD), BF),
            pltpu.VMEM((16, 64, 2 * HD), BF),
            pltpu.VMEM((16, 16, 512), BF),
            pltpu.VMEM((16, 16, 512), BF),
            pltpu.VMEM((16, 512), BF),
            pltpu.VMEM((16, 16, 512), BF),
            pltpu.VMEM((4, D, HD), BF),
            pltpu.VMEM((4, HD, D), BF),
            pltpu.VMEM((4, 64, 512), F32),
            pltpu.VMEM((16, 16, 512), BF),
            pltpu.VMEM((16, 16, 512), BF),
            dma((3,)),
            dma((2, 4)),
            dma((2, 4)),
            dma((2, 8)),
            dma((2, 8)),
            dma((2, 8)),
            dma((2, 8)),
        ]
        + [dma((16,))] * 18
        + [dma((2,)), dma((2,)), dma((2,)), dma((2, 4)), dma((2, 4)), dma((2, 4)), dma((2, 4))],
        compiler_params=pltpu.CompilerParams(
            collective_id=0, has_side_effects=True, vmem_limit_bytes=VLIMIT
        ),
    )(
        latent_offset, jnp.sin(angles), jnp.cos(angles), token_ids.reshape(4, 128), embed_table,
        cross_q, cross_kv, cross_out, self_qkv, self_out, mlp_in, mlp_out,
    )
    return rows.astype(BF)[None]


def solution(mesh):
    placed = (
        P("ctx"),
        P(),
        P(),
        P("ctx", "lat"),
        P(None, "ctx", "lat"),
        P("lat", None),
        P(None, None, "lat"),
        P("lat", None),
        P(None, "ctx"),
        P("ctx", None),
    )
    return jax.shard_map(
        per_device, mesh=mesh, in_specs=placed, out_specs=P("lat", "ctx", None), check_vma=False
    )
```

time: 533 us -> 130 us (0.24)
  blocking collectives: 163 us -> 0 us
  waiting for transfers between devices: 157 us -> 0 us
  Pallas kernels: 0 us -> 125 us
  local copies, waits for them, and re-layouts: 81.4 us -> 0.01 us
  matrix products: 52.1 us -> 0 us
  other arithmetic: 48.5 us -> 4.03 us
  between operations: 14.3 us -> 0.68 us
  starting transfers between devices: 10.7 us -> 0 us
    all_to_all x4 -> x0, blocking collectives: 163 us -> none  [the longest x1 72.6 us: side_by_side(): lax.all_to_all(both, axis, split_axis=split_dim, concat_axis=concat_dim,...]
    all_gather x3 -> x0, waiting for transfers between devices: 147 us -> none  [the longest x1 76.2 us: per_device(): gathered = lax.all_gather(mlp_normed, 'ctx', axis=0, tiled=True)]
    pallas_call x0 -> x1, Pallas kernels: none -> 125 us  [per_device(): pl.pallas_call(whole_kernel, out_shape=jax.ShapeDtypeStruct((4, D), F32),...]
    dot_general x27 -> x0, matrix products: 52.1 us -> none  [the longest x8 10.6 us: one_head(): lax.dot_general(query, key, (((1,), (1,)), ((), ())), preferred_element_t...]
    reshape x11 -> x0, local copies, waits for them, and re-layouts: 39 us -> none  [the longest x4 31.9 us: sinusoid(): jnp.stack([jnp.sin(angles), jnp.cos(angles)], axis=-1)]
    sin x2 -> x0, other arithmetic: 22.2 us -> none  [sinusoid(): jnp.sin(angles)]
    another operation x2 -> x0, local copies, waits for them, and re-layouts: 20.7 us -> none  [sinusoid(): jnp.stack([jnp.sin(angles), jnp.cos(angles)], axis=-1)]
    reduce_sum x15 -> x0, other arithmetic: 10.9 us -> none  [the longest x8 3.13 us: one_head(): total = jnp.sum(weights.astype(jnp.float32), axis=1)]
  transfers between devices with their start and end apart: 5 -> 0, of which waited for: 3 -> 0; matrix products, arithmetic and copies ran while one was open for 20% -> 0% of each run, Pallas kernels for 0% -> 0%
where the time goes in v2:
time: 130 us
  Pallas kernels  125 us (96%)
  other arithmetic  4.03 us (3%)
    pallas_call x1, Pallas kernels, per_device(): pl.pallas_call(whole_kernel, out_shape=jax.ShapeDtypeStruct((4, D), F32),...  125 us

profile of v2, /device:TPU:1, one launch (start us, length us, event | category | flops | bytes accessed | tf_op | source)
XLA Modules:
  0.0 129.8 jit_solution(6028602562386866644)
XLA Ops:
  0.7 0.1 add_convert_fusion
  0.8 2.6 %multiply_cosine_fusion = (f32[56,2048]{1,0:T(8,128)}, f32[56,2048]{1,0:T(8,128)}) fusion(f32[2048]{0:T(1024)S(1)} %fusion.2, f32[56]{0:T(128)S(1)} %add_convert_fusion), kind=kLoop, calls=%fused_computation | loop fusion | flops 114688 | bytes 925920 | tf_op jit(solution)/shard_map/cos | solution.py:610
  3.3 125.1 %shard_map.100 = f32[4,2048]{1,0:T(4,128)} custom-call(s32[1]{0:T(128)} %copy.11.offset_ref, f32[56,2048]{1,0:T(8,128)} %get-tuple-element.6.sin_ref, f32[56,2048]{1,0:T(8,128)} %get-tuple-element.5.cos_ref, s32[4,128]{1,0:T(4,128)} %bitcast.5, bf16[256,2048]{1,0:T(8,128)(2,1)} %table_ref.1, bf16[32,512]{1,0:T(8,128)(2,1)} %q_ref.1, ...), custom_call_target="tpu_custom_call" | custom-call | tf_op jit(solution)/shard_map/pallas_call | solution.py:552
  128.4 1.4 %convert_bitcast_fusion = bf16[1,4,2048]{2,1,0:T(4,128)(2,1)} fusion(f32[4,2048]{1,0:T(4,128)} %shard_map.100), kind=kLoop, calls=%fused_computation.2 | loop fusion | flops 8192 | bytes 49152 | tf_op jit(solution)/shard_map/broadcast_in_dim | solution.py:613
  (4 shorter events, 0.0 us)

commit v3 on v2

--- a/solution.py
+++ b/solution.py
@@ -88,10 +88,10 @@
 
 
 def whole_kernel(
-    offset_ref, sin_ref, cos_ref, tok_ref, table_ref, q_ref, kv_ref,
+    offset_ref, tok_ref, table_ref, q_ref, kv_ref,
     cout_ref, sqkv_ref, sout_ref, in_ref, mout_ref,
     out_ref,
-    stage, w_all, tokens, wkv, tw, rows_sin, rows_cos, waves, one_hot, inverse, latent, keys, values, q_own, q_all,
+    stage, w_all, tokens, wkv, tw, sin_ref, cos_ref, rows_sin, rows_cos, waves, products, one_hot, inverse, latent, keys, values, q_own, q_all,
     o_msg, o_came, st_msg, st_came, w_co, w_qkv, w_so, msg, came, own, all_rows, normed, kv, kv_all, msg2, came2,
     own2, all_rows2, w_in, w_out, partial, msg3, came3,
     load, s1, r1, s2, r2, s3, r3, s_q, r_q, s_o, r_o, s_st, r_st, s_m, r_m, s_a, r_a, s_kv, r_kv, s_m2, r_m2,
@@ -145,7 +145,43 @@
         stage[h, 0] = q_ref[:, 128 * h : 128 * h + 128]
         stage[h, 1] = kv_ref[0, :, 128 * h : 128 * h + 128]
         stage[h, 2] = kv_ref[1, :, 128 * h : 128 * h + 128]
+    offset = offset_ref[0]
+    index = lax.broadcasted_iota(jnp.int32, (56, 1), 0)
+    places = jnp.where(index < 4, 512 * (16 * x + 4 * index + k), offset + 256 * (index - 4) + 16 * r)
+    places = jnp.where(index < 8, places, jnp.where(index < 40, 16 * (index - 8), index - 40)).astype(F32)
+
+    def table_columns(j):
+        lanes = pl.ds(pl.multiple_of(j * 256, 256), 256)
+        pair = ((j * 256 + lax.broadcasted_iota(jnp.int32, (1, 256), 1)) // 2).astype(F32)
+        angles = places * jnp.exp(pair * (-2.0 * math.log(10000.0) / D))
+        sin_ref[:, lanes] = jnp.sin(angles)
+        cos_ref[:, lanes] = jnp.cos(angles)
+
+    each(0, 8, table_columns)
+    odd = lax.broadcasted_iota(jnp.int32, (1, D), 1) % 2 == 1
+    mid_sin, mid_cos = sin_ref[8:40], cos_ref[8:40]
+
+    def start_of(n):
+        s, co = sin_ref[pl.ds(n, 1)], cos_ref[pl.ds(n, 1)]
+        return jnp.where(odd, co, s), jnp.where(odd, -s, co)
+
+    def waves_of(n):
+        s, co = start_of(n)
+        rows_sin[...] = s * mid_cos + co * mid_sin
+        rows_cos[...] = co * mid_cos - s * mid_sin
+
+        def columns(j):
+            lanes = pl.ds(pl.multiple_of(j * 128, 128), 128)
+            low_sin, low_cos = sin_ref[40:56, lanes], cos_ref[40:56, lanes]
+            for m in range(32):
+                wave = rows_sin[m : m + 1, lanes] * low_cos + rows_cos[m : m + 1, lanes] * low_sin
+                waves[pl.ds(pl.multiple_of(n * 512 + 16 * m, 16), 16), lanes] = wave.astype(BF)
+
+        each(0, 16, columns)
+
+    each(0, 4, waves_of)
     pl.semaphore_wait(barrier, jnp.where(a == k, 45, 46))
+    ends = []
 
     heads = [(a + d) % 4 for d in range(1, 4)]
     rows = [((x + dx) % 4, (b + db) % 2) for dx in (0, 1, 3, 2) for db in (0, 1) if dx or db]
@@ -156,32 +192,27 @@
         first_copies.append(push(stage.at[h], w_all.at[:, x, a, k], s1.at[0, h], r1.at[0, a], there))
     for copy in first_copies:
         copy.start()
+        ends.append(copy.wait_send)
     tokens[x, a, k] = tok_ref[...]
     for part in range(3):
         w_all[part, x, a, k] = stage[a, part]
 
-    odd = lax.broadcasted_iota(jnp.int32, (1, D), 1) % 2 == 1
-    mid_sin, mid_cos = sin_ref[8:40], cos_ref[8:40]
-
-    def start_of(n):
-        s, co = sin_ref[pl.ds(n, 1)], cos_ref[pl.ds(n, 1)]
-        return jnp.where(odd, co, s), jnp.where(odd, -s, co)
-
-    def waves_of(n):
-        s, co = start_of(n)
-        rows_sin[...] = s * mid_cos + co * mid_sin
-        rows_cos[...] = co * mid_cos - s * mid_sin
-
-        def columns(j):
-            lanes = pl.ds(pl.multiple_of(j * 128, 128), 128)
-            low_sin, low_cos = sin_ref[40:56, lanes], cos_ref[40:56, lanes]
-            for m in range(32):
-                wave = rows_sin[m : m + 1, lanes] * low_cos + rows_cos[m : m + 1, lanes] * low_sin
-                waves[pl.ds(pl.multiple_of(n * 512 + 16 * m, 16), 16), lanes] = wave.astype(BF)
-
-        each(0, 16, columns)
-
-    each(0, 4, waves_of)
+    square = table_ref[...].astype(F32)
+    square = square * square
+    high = square.astype(BF)
+    lower = (square - high.astype(F32)).astype(BF)
+    ones = jnp.ones((8, D), BF)
+    across = (((1,), (1,)), ((), ()))
+    norms = lax.dot_general(ones, high, across, preferred_element_type=F32) + lax.dot_general(
+        ones, lower, across, preferred_element_type=F32
+    )
+    norms = norms[0:1]
+
+    def products_of(n):
+        run = pl.ds(pl.multiple_of(n * 512, 512), 512)
+        products[run, :] = lax.dot_general(waves[run, :], table_ref[...], across, preferred_element_type=F32)
+
+    each(0, 4, products_of)
 
     for h in heads:
         arrive(tokens.at[x, h, k], r1.at[1, h], partner)
@@ -194,6 +225,7 @@
         second_copies.append(push(w_all.at[:, x, :, k], w_all.at[:, x, :, k], s2.at[0, j], r2.at[0, j_me], there))
     for copy in second_copies:
         copy.start()
+        ends.append(copy.wait_send)
 
     def onward(rx, rb):
         j = 2 * rx + rb
@@ -206,52 +238,7 @@
     third_copies = onward(x, b)
     for copy in third_copies:
         copy.start()
-
-    square = table_ref[...].astype(F32)
-    square = square * square
-    high = square.astype(BF)
-    lower = (square - high.astype(F32)).astype(BF)
-    ones = jnp.ones((8, D), BF)
-    across = (((1,), (1,)), ((), ()))
-    norms = lax.dot_general(ones, high, across, preferred_element_type=F32) + lax.dot_general(
-        ones, lower, across, preferred_element_type=F32
-    )
-    norms = norms[0:1]
-    vocab = lax.broadcasted_iota(jnp.int32, (128, 256), 1).astype(F32)
-    diagonal = lax.broadcasted_iota(jnp.int32, (128, 128), 0) == lax.broadcasted_iota(jnp.int32, (128, 128), 1)
-
-    def scales_of(n):
-        here = tokens[x, n, k].astype(F32)
-        row = pl.multiple_of(n * 512, 512)
-        products = lax.dot_general(waves[pl.ds(row, 512), :], table_ref[...], across, preferred_element_type=F32)
-        for q in range(4):
-            column = jnp.sum(jnp.where(diagonal, here[q : q + 1, :], 0.0), axis=1, keepdims=True)
-            chosen = column == vocab
-            quarter = pl.ds(pl.multiple_of(n * 512 + 128 * q, 128), 128)
-            one_hot[quarter, :] = chosen.astype(BF)
-            total = jnp.sum(
-                jnp.where(chosen, 2.0 * products[128 * q : 128 * q + 128] + norms, 0.0), axis=1, keepdims=True
-            )
-            total = jnp.maximum(total + D / 2, 0.0)
-            inverse[quarter, :] = lax.rsqrt(total * (1.0 / D) + EPSILON)
-
-    each(0, 4, scales_of)
-
-    for rx, rb in rows:
-        sx, sb = (2 * x + 4 - rx) % 4, rb
-        j = 2 * sx + sb
-        k2 = 2 * sb + c
-        arrive(tokens.at[sx, :, k2], r2.at[1, j], partner)
-        arrive(w_all.at[:, sx, :, k2], r2.at[0, j], partner)
-        more = onward(sx, sb)
-        for copy in more:
-            copy.start()
-        third_copies += more
-    for rx, rb in [(x, b)] + rows:
-        j = 2 * rx + rb
-        k3 = 2 * rb + 1 - c
-        arrive(tokens.at[rx, :, k3], r3.at[1, j], partner)
-        arrive(w_all.at[:, rx, :, k3], r3.at[0, j], partner)
+        ends.append(copy.wait_send)
 
     main = c == y // 2
     source = jnp.logical_and(main, b == y % 2)
@@ -270,7 +257,40 @@
         for copy in step1 + mine:
             copy.start()
 
-    offset = offset_ref[0]
+    vocab = lax.broadcasted_iota(jnp.int32, (128, 256), 1).astype(F32)
+    diagonal = lax.broadcasted_iota(jnp.int32, (128, 128), 0) == lax.broadcasted_iota(jnp.int32, (128, 128), 1)
+
+    def scales_of(n):
+        here = tokens[x, n, k].astype(F32)
+        for q in range(4):
+            column = jnp.sum(jnp.where(diagonal, here[q : q + 1, :], 0.0), axis=1, keepdims=True)
+            chosen = column == vocab
+            quarter = pl.ds(pl.multiple_of(n * 512 + 128 * q, 128), 128)
+            one_hot[quarter, :] = chosen.astype(BF)
+            total = jnp.sum(
+                jnp.where(chosen, 2.0 * products[quarter, :] + norms, 0.0), axis=1, keepdims=True
+            )
+            total = jnp.maximum(total + D / 2, 0.0)
+            inverse[quarter, :] = lax.rsqrt(total * (1.0 / D) + EPSILON)
+
+    each(0, 4, scales_of)
+
+    for rx, rb in rows:
+        sx, sb = (2 * x + 4 - rx) % 4, rb
+        j = 2 * sx + sb
+        k2 = 2 * sb + c
+        arrive(tokens.at[sx, :, k2], r2.at[1, j], partner)
+        arrive(w_all.at[:, sx, :, k2], r2.at[0, j], partner)
+        more = onward(sx, sb)
+        for copy in more:
+            copy.start()
+            ends.append(copy.wait_send)
+    for rx, rb in [(x, b)] + rows:
+        j = 2 * rx + rb
+        k3 = 2 * rb + 1 - c
+        arrive(tokens.at[rx, :, k3], r3.at[1, j], partner)
+        arrive(w_all.at[:, rx, :, k3], r3.at[0, j], partner)
+
     slot = lax.broadcasted_iota(jnp.int32, (64, 1), 0)
     target = offset + (slot // 16) * 256 + 16 * r + slot % 16
     lane = lax.broadcasted_iota(jnp.int32, (1, 128), 1)
@@ -290,6 +310,7 @@
     q_own[...] = jnp.dot(latent[...], weights_of[0], preferred_element_type=F32).astype(BF)
     asked = Exchange(q_own, q_all, s_q, r_q, r, row_of, 16, whole=True)
     asked.start()
+    ends.append(asked.wait_sent)
 
     wkv[:, :HD] = weights_of[1]
     wkv[:, HD:] = weights_of[2]
@@ -343,33 +364,46 @@
     st_came[r] = st_msg[r]
     stats.wait_all()
     outs.wait_all()
-
-    def forward(i):
-        return [
-            push(w_in.at[i], w_in.at[i], sw3.at[0, i], rw3.at[0, i], partner),
-            push(w_out.at[i], w_out.at[i], sw3.at[1, i], rw3.at[1, i], partner),
-        ]
-
-    step2 = []
-    for d in (1, 3, 2):
-        there = at((x + d) % 4, a, b, c, y)
-        step2.append(push(w_in.at[x], w_in.at[x], sw2.at[0, d], rw2.at[0, x], there))
-        step2.append(push(w_out.at[x], w_out.at[x], sw2.at[1, d], rw2.at[1, x], there))
-
-    @pl.when(source)
-    def _():
-        for copy in mine:
-            copy.wait()
-
-    @pl.when(jnp.logical_and(main, jnp.logical_not(source)))
-    def _():
-        arrive(w_in.at[x], rw1.at[0], partner)
-        arrive(w_out.at[x], rw1.at[1], partner)
-
-    @pl.when(main)
-    def _():
-        for copy in step2 + forward(x):
-            copy.start()
+    ends += [stats.wait_sent, outs.wait_sent]
+
+    halves = (w_in, w_out)
+    others = [(x + d) % 4 for d in (1, 3, 2)]
+
+    def along(h):
+        copies = [push(halves[h].at[x], halves[h].at[x], sw2.at[h, i], rw2.at[h, x], at(i, a, b, c, y)) for i in others]
+        return copies + [forward(h, x)]
+
+    def forward(h, i):
+        return push(halves[h].at[i], halves[h].at[i], sw3.at[h, i], rw3.at[h, i], partner)
+
+    def set_out(h):
+        @pl.when(source)
+        def _():
+            mine[h].wait()
+
+        @pl.when(jnp.logical_and(main, jnp.logical_not(source)))
+        def _():
+            arrive(halves[h].at[x], rw1.at[h], partner)
+
+        @pl.when(main)
+        def _():
+            for copy in along(h):
+                copy.start()
+
+    def hand_over(h):
+        @pl.when(main)
+        def _():
+            for i in others:
+                arrive(halves[h].at[i], rw2.at[h, i], partner)
+                forward(h, i).start()
+
+    def receive(h):
+        @pl.when(jnp.logical_not(main))
+        def _():
+            for i in range(4):
+                arrive(halves[h].at[i], rw3.at[h, i], partner)
+
+    set_out(0)
 
     maxima, totals = st_came[:, 0, :], st_came[:, 1, :]
     factor = jnp.exp(maxima - jnp.max(maxima, axis=0, keepdims=True))
@@ -398,11 +432,13 @@
     own_block = (pl.ds(pl.multiple_of(16 * y, 16), 16), pl.ds(pl.multiple_of(512 * a, 512), 512))
     own_latent = latent[own_block].astype(F32)
     summed.wait_all()
+    ends.append(summed.wait_sent)
     first = jnp.sum(came[...].astype(F32), axis=0) + own_latent
     own[...] = first.astype(BF)
     spread = Exchange(own, all_rows, s_a, r_a, p, head_of, 16, whole=True)
     spread.start()
     spread.wait_all()
+    ends.append(spread.wait_sent)
 
     rows_normed(all_rows)
     kv[:, :HD] = jnp.dot(normed[...], w_qkv[1], preferred_element_type=F32).astype(BF)
@@ -411,16 +447,10 @@
     both.start()
     query = jnp.dot(normed[...], w_qkv[0], preferred_element_type=F32).astype(BF)
     both.wait_all()
-
-    @pl.when(main)
-    def _():
-        for d in (1, 3, 2):
-            i = (x + d) % 4
-            arrive(w_in.at[i], rw2.at[0, i], partner)
-            arrive(w_out.at[i], rw2.at[1, i], partner)
-            for copy in forward(i):
-                copy.start()
-
+    ends.append(both.wait_sent)
+
+    set_out(1)
+    hand_over(0)
     all_keys = kv_all[:, :, :HD].reshape(LATENTS, HD)
     all_values = kv_all[:, :, HD:].reshape(LATENTS, HD)
     scores = lax.dot_general(query, all_keys, across, preferred_element_type=F32) * SCALE
@@ -436,25 +466,24 @@
     summed2 = Exchange(msg2, came2, s_m2, r_m2, p, head_of, 16)
     summed2.start()
     summed2.wait_all()
+    ends.append(summed2.wait_sent)
     second = first + jnp.sum(came2[...].astype(F32), axis=0)
     own2[...] = second.astype(BF)
     spread2 = Exchange(own2, all_rows2, s_a2, r_a2, p, head_of, 16, whole=True)
     spread2.start()
 
-    @pl.when(jnp.logical_not(main))
-    def _():
-        for i in range(4):
-            arrive(w_in.at[i], rw3.at[0, i], partner)
-            arrive(w_out.at[i], rw3.at[1, i], partner)
-
     spread2.wait_all()
+    ends.append(spread2.wait_sent)
 
     rows_normed(all_rows2)
+    hand_over(1)
+    receive(0)
     hidden = []
     for i in range(4):
         pre = jnp.dot(normed[...], w_in[i], preferred_element_type=F32)
         hidden.append(jax.nn.gelu(pre, approximate=True).astype(BF))
     hidden = jnp.concatenate(hidden, axis=1)
+    receive(1)
     for q in range(4):
         columns = slice(512 * q, 512 * q + 512)
         partial[q] = jnp.dot(hidden, w_out[:, :, columns].reshape(512, 512), preferred_element_type=F32)
@@ -492,10 +521,8 @@
     for q in range(4):
         out_ref[:, 512 * q : 512 * q + 512] = ended[4 * q : 4 * q + 4]
 
-    for copy in first_copies + second_copies + third_copies:
-        copy.wait_send()
-    for exchange in (asked, outs, stats, summed, spread, both, summed2, spread2):
-        exchange.wait_sent()
+    for end in ends:
+        end()
 
     def last_sent(i):
         j = (p + i) % 16
@@ -513,11 +540,11 @@
 
     @pl.when(main)
     def _():
-        for copy in step2:
-            copy.wait_send()
-        for i in range(4):
-            for copy in forward(i):
+        for h in range(2):
+            for copy in along(h):
                 copy.wait_send()
+            for i in others:
+                forward(h, i).wait_send()
 
 
 def per_device(
@@ -532,27 +559,13 @@
     mlp_in,
     mlp_out,
 ):
-    x, a, b, c, y = place()
-    r = 4 * x + 2 * b + c
-    feature = jnp.arange(D, dtype=jnp.int32)
-    rates = jnp.exp((feature // 2).astype(F32) * (-2.0 * math.log(10000.0) / D))
-    four = jnp.arange(4, dtype=jnp.int32)
-    places = jnp.concatenate(
-        [
-            512 * (16 * x + 4 * four + 2 * b + c),
-            latent_offset[0] + 256 * four + 16 * r,
-            16 * jnp.arange(32, dtype=jnp.int32),
-            jnp.arange(16, dtype=jnp.int32),
-        ]
-    )
-    angles = places.astype(F32)[:, None] * rates[None, :]
     vmem = pl.BlockSpec(memory_space=pltpu.VMEM)
     hbm = pl.BlockSpec(memory_space=pl.ANY)
     dma = pltpu.SemaphoreType.DMA
     rows = pl.pallas_call(
         whole_kernel,
         out_shape=jax.ShapeDtypeStruct((4, D), F32),
-        in_specs=[pl.BlockSpec(memory_space=pltpu.SMEM)] + [vmem] * 6 + [hbm] * 5,
+        in_specs=[pl.BlockSpec(memory_space=pltpu.SMEM)] + [vmem] * 4 + [hbm] * 5,
         out_specs=vmem,
         scratch_shapes=[
             pltpu.VMEM((4, 3, 32, HD), BF),
@@ -560,9 +573,12 @@
             pltpu.VMEM((4, 4, 4, 4, 128), jnp.int32),
             pltpu.VMEM((D, 2 * HD), BF),
             pltpu.VMEM((2, 256, 2 * HD), BF),
+            pltpu.VMEM((56, D), F32),
+            pltpu.VMEM((56, D), F32),
             pltpu.VMEM((32, D), F32),
             pltpu.VMEM((32, D), F32),
             pltpu.VMEM((2048, D), BF),
+            pltpu.VMEM((2048, 256), F32),
             pltpu.VMEM((2048, 256), BF),
             pltpu.VMEM((2048, 1), F32),
             pltpu.VMEM((64, D), BF),
@@ -607,7 +623,7 @@
             collective_id=0, has_side_effects=True, vmem_limit_bytes=VLIMIT
         ),
     )(
-        latent_offset, jnp.sin(angles), jnp.cos(angles), token_ids.reshape(4, 128), embed_table,
+        latent_offset, token_ids.reshape(4, 128), embed_table,
         cross_q, cross_kv, cross_out, self_qkv, self_out, mlp_in, mlp_out,
     )
     return rows.astype(BF)[None]

time: 130 us -> 121 us (0.931)
  Pallas kernels: 125 us -> 119 us
  other arithmetic: 4.03 us -> 1.37 us
    pallas_call x1, Pallas kernels: 125 us -> 119 us  [per_device(): pl.pallas_call(whole_kernel, out_shape=jax.ShapeDtypeStruct((4, D), F32),...]
    cos x1 -> x0, other arithmetic: 2.56 us -> none  [per_device(): jnp.cos(angles)]
where the time goes in v3:
time: 121 us
  Pallas kernels  119 us (98%)
  other arithmetic  1.37 us (1%)
    pallas_call x1, Pallas kernels, per_device(): pl.pallas_call(whole_kernel, out_shape=jax.ShapeDtypeStruct((4, D), F32),...  119 us

profile of v3, /device:TPU:1, one launch (start us, length us, event | category | flops | bytes accessed | tf_op | source)
XLA Modules:
  0.0 120.5 jit_solution(1028453333829143028)
XLA Ops:
  0.7 118.5 %shard_map.100 = f32[4,2048]{1,0:T(4,128)} custom-call(s32[1]{0:T(128)S(6)} %copy.11.offset_ref, s32[4,128]{1,0:T(4,128)} %bitcast.3, bf16[256,2048]{1,0:T(8,128)(2,1)} %table_ref.1, bf16[32,512]{1,0:T(8,128)(2,1)} %q_ref.1, bf16[2,32,512]{2,1,0:T(8,128)(2,1)} %kv_ref.1, bf16[512,2048]{1,0:T(8,128)(2,1)} %cout_ref.1, bf16[3,2048,512]{2,1,0:T(8,128)(2,1)} %sqkv_ref.1, ...), custom_call_target="tpu_custom_call" | custom-call | tf_op jit(solution)/shard_map/pallas_call | solution.py:565
  119.2 1.4 %convert_bitcast_fusion = bf16[1,4,2048]{2,1,0:T(4,128)(2,1)} fusion(f32[4,2048]{1,0:T(4,128)} %shard_map.100), kind=kLoop, calls=%fused_computation | loop fusion | flops 8192 | bytes 49152 | tf_op jit(solution)/shard_map/broadcast_in_dim | solution.py:629

commit v4 on v3

--- a/solution.py
+++ b/solution.py
@@ -91,7 +91,7 @@
     offset_ref, tok_ref, table_ref, q_ref, kv_ref,
     cout_ref, sqkv_ref, sout_ref, in_ref, mout_ref,
     out_ref,
-    stage, w_all, tokens, wkv, tw, sin_ref, cos_ref, rows_sin, rows_cos, waves, products, one_hot, inverse, latent, keys, values, q_own, q_all,
+    stage, w_all, tokens, wkv, table_w, tw, sin_ref, cos_ref, rows_sin, rows_cos, waves, products, one_hot, inverse, latent, keys, values, q_own, q_all,
     o_msg, o_came, st_msg, st_came, w_co, w_qkv, w_so, msg, came, own, all_rows, normed, kv, kv_all, msg2, came2,
     own2, all_rows2, w_in, w_out, partial, msg3, came3,
     load, s1, r1, s2, r2, s3, r3, s_q, r_q, s_o, r_o, s_st, r_st, s_m, r_m, s_a, r_a, s_kv, r_kv, s_m2, r_m2,
@@ -132,7 +132,6 @@
     def hello(device):
         pl.semaphore_signal(barrier, inc=1, device_id=device, device_id_type=MESH)
 
-    each(1, 16, lambda i: hello(row_of((r + i) % 16)))
     each(1, 16, lambda i: hello(head_of((p + i) % 16)))
 
     def hello_sender(j):
@@ -141,6 +140,7 @@
             hello(sender_of(j))
 
     each(0, 16, hello_sender)
+    each(1, 16, lambda i: hello(row_of((r + i) % 16)))
     for h in range(4):
         stage[h, 0] = q_ref[:, 128 * h : 128 * h + 128]
         stage[h, 1] = kv_ref[0, :, 128 * h : 128 * h + 128]
@@ -180,23 +180,6 @@
         each(0, 16, columns)
 
     each(0, 4, waves_of)
-    pl.semaphore_wait(barrier, jnp.where(a == k, 45, 46))
-    ends = []
-
-    heads = [(a + d) % 4 for d in range(1, 4)]
-    rows = [((x + dx) % 4, (b + db) % 2) for dx in (0, 1, 3, 2) for db in (0, 1) if dx or db]
-    first_copies = []
-    for h in heads:
-        there = at(x, h, b, c, y)
-        first_copies.append(push(tok_ref, tokens.at[x, a, k], s1.at[1, h], r1.at[1, a], there))
-        first_copies.append(push(stage.at[h], w_all.at[:, x, a, k], s1.at[0, h], r1.at[0, a], there))
-    for copy in first_copies:
-        copy.start()
-        ends.append(copy.wait_send)
-    tokens[x, a, k] = tok_ref[...]
-    for part in range(3):
-        w_all[part, x, a, k] = stage[a, part]
-
     square = table_ref[...].astype(F32)
     square = square * square
     high = square.astype(BF)
@@ -213,49 +196,53 @@
         products[run, :] = lax.dot_general(waves[run, :], table_ref[...], across, preferred_element_type=F32)
 
     each(0, 4, products_of)
+    pl.semaphore_wait(barrier, jnp.where(a == k, 45, 46))
+    ends = []
+
+    heads = [(a + d) % 4 for d in range(1, 4)]
+    rows = [((x + dx) % 4, (b + db) % 2) for dx in (0, 1, 3, 2) for db in (0, 1) if dx or db]
+    early, late = pl.ds(0, 1), pl.ds(1, 2)
+
+    def begin(copies):
+        for copy in copies:
+            copy.start()
+            ends.append(copy.wait_send)
+
+    begin([push(tok_ref, tokens.at[x, a, k], s1.at[2, h], r1.at[2, a], at(x, h, b, c, y)) for h in heads])
+    for n, part in enumerate((early, late)):
+        begin(
+            [
+                push(stage.at[h, part], w_all.at[part, x, a, k], s1.at[n, h], r1.at[n, a], at(x, h, b, c, y))
+                for h in heads
+            ]
+        )
+    tokens[x, a, k] = tok_ref[...]
+    for part in range(3):
+        w_all[part, x, a, k] = stage[a, part]
 
     for h in heads:
-        arrive(tokens.at[x, h, k], r1.at[1, h], partner)
-        arrive(w_all.at[:, x, h, k], r1.at[0, h], partner)
-    second_copies = []
-    for rx, rb in rows:
-        there = at(rx, a, rb, c, y)
+        arrive(tokens.at[x, h, k], r1.at[2, h], partner)
+        arrive(w_all.at[early, x, h, k], r1.at[0, h], partner)
+        arrive(w_all.at[late, x, h, k], r1.at[1, h], partner)
+
+    def piece(n, rx, rb, core):
+        k2 = 2 * rb + core
+        if n == 2:
+            return tokens.at[rx, :, k2]
+        return w_all.at[(early, late)[n], rx, :, k2]
+
+    def along_rows(n):
+        return [
+            push(piece(n, x, b, c), piece(n, x, b, c), s2.at[n, 2 * rx + rb], r2.at[n, j_me], at(rx, a, rb, c, y))
+            for rx, rb in rows
+        ]
+
+    def onward(n, rx, rb):
         j = 2 * rx + rb
-        second_copies.append(push(tokens.at[x, :, k], tokens.at[x, :, k], s2.at[1, j], r2.at[1, j_me], there))
-        second_copies.append(push(w_all.at[:, x, :, k], w_all.at[:, x, :, k], s2.at[0, j], r2.at[0, j_me], there))
-    for copy in second_copies:
-        copy.start()
-        ends.append(copy.wait_send)
-
-    def onward(rx, rb):
-        j = 2 * rx + rb
-        k2 = 2 * rb + c
-        return [
-            push(tokens.at[rx, :, k2], tokens.at[rx, :, k2], s3.at[1, j], r3.at[1, j], partner),
-            push(w_all.at[:, rx, :, k2], w_all.at[:, rx, :, k2], s3.at[0, j], r3.at[0, j], partner),
-        ]
-
-    third_copies = onward(x, b)
-    for copy in third_copies:
-        copy.start()
-        ends.append(copy.wait_send)
-
-    main = c == y // 2
-    source = jnp.logical_and(main, b == y % 2)
-    beside = at(x, a, 1 - b, c, y)
-    mine = [
-        pltpu.make_async_copy(in_ref, w_in.at[x], own_w.at[0]),
-        pltpu.make_async_copy(mout_ref, w_out.at[x], own_w.at[1]),
-    ]
-    step1 = [
-        push(in_ref, w_in.at[x], sw1.at[0], rw1.at[0], beside),
-        push(mout_ref, w_out.at[x], sw1.at[1], rw1.at[1], beside),
-    ]
-
-    @pl.when(source)
-    def _():
-        for copy in step1 + mine:
-            copy.start()
+        return push(piece(n, rx, rb, c), piece(n, rx, rb, c), s3.at[n, j], r3.at[n, j], partner)
+
+    for n in (2, 0, 1):
+        begin(along_rows(n) + [onward(n, x, b)])
 
     vocab = lax.broadcasted_iota(jnp.int32, (128, 256), 1).astype(F32)
     diagonal = lax.broadcasted_iota(jnp.int32, (128, 128), 0) == lax.broadcasted_iota(jnp.int32, (128, 128), 1)
@@ -275,21 +262,19 @@
 
     each(0, 4, scales_of)
 
+    def hand_on(n, rx, rb):
+        arrive(piece(n, rx, rb, c), r2.at[n, 2 * rx + rb], partner)
+        begin([onward(n, rx, rb)])
+
+    def handed(n, rx, rb):
+        arrive(piece(n, rx, rb, 1 - c), r3.at[n, 2 * rx + rb], partner)
+
     for rx, rb in rows:
-        sx, sb = (2 * x + 4 - rx) % 4, rb
-        j = 2 * sx + sb
-        k2 = 2 * sb + c
-        arrive(tokens.at[sx, :, k2], r2.at[1, j], partner)
-        arrive(w_all.at[:, sx, :, k2], r2.at[0, j], partner)
-        more = onward(sx, sb)
-        for copy in more:
-            copy.start()
-            ends.append(copy.wait_send)
+        hand_on(2, (2 * x + 4 - rx) % 4, rb)
+        hand_on(0, (2 * x + 4 - rx) % 4, rb)
     for rx, rb in [(x, b)] + rows:
-        j = 2 * rx + rb
-        k3 = 2 * rb + 1 - c
-        arrive(tokens.at[rx, :, k3], r3.at[1, j], partner)
-        arrive(w_all.at[:, rx, :, k3], r3.at[0, j], partner)
+        handed(2, rx, rb)
+        handed(0, rx, rb)
 
     slot = lax.broadcasted_iota(jnp.int32, (64, 1), 0)
     target = offset + (slot // 16) * 256 + 16 * r + slot % 16
@@ -306,22 +291,62 @@
         s, co = start_of(4 + t)
         wave = s * cos_ref[40:56] + co * sin_ref[40:56]
         latent[16 * t : 16 * t + 16, :] = rms_rows(looked[16 * t : 16 * t + 16] + wave).astype(BF)
-    weights_of = w_all.reshape(3, D, HD)
-    q_own[...] = jnp.dot(latent[...], weights_of[0], preferred_element_type=F32).astype(BF)
+    q_own[...] = jnp.dot(latent[...], w_all[0].reshape(D, HD), preferred_element_type=F32).astype(BF)
     asked = Exchange(q_own, q_all, s_q, r_q, r, row_of, 16, whole=True)
     asked.start()
-    ends.append(asked.wait_sent)
-
-    wkv[:, :HD] = weights_of[1]
-    wkv[:, HD:] = weights_of[2]
-    table_w = jnp.dot(table_ref[...], wkv[...], preferred_element_type=F32)
-    tw[0] = table_w.astype(BF)
-    tw[1] = (table_w - table_w.astype(BF).astype(F32)).astype(BF)
+
+    main = c == y // 2
+    source = jnp.logical_and(main, b == y % 2)
+    beside = at(x, a, 1 - b, c, y)
+    mine = [
+        pltpu.make_async_copy(in_ref, w_in.at[x], own_w.at[0]),
+        pltpu.make_async_copy(mout_ref, w_out.at[x], own_w.at[1]),
+    ]
+    step1 = [
+        push(in_ref, w_in.at[x], sw1.at[0], rw1.at[0], beside),
+        push(mout_ref, w_out.at[x], sw1.at[1], rw1.at[1], beside),
+    ]
+
+    def set_first():
+        @pl.when(source)
+        def _():
+            for copy in step1 + mine:
+                copy.start()
+
+    for d in (0, 1, 3, 2):
+        sx = (x + d) % 4
+        if d == 0:
+            hand_on(1, x, 1 - b)
+            handed(1, x, b)
+            handed(1, x, 1 - b)
+        else:
+            for rb in (0, 1):
+                hand_on(1, sx, rb)
+            for rb in (0, 1):
+                handed(1, sx, rb)
+        if d == 2:
+            ends.append(asked.wait_sent)
+        if d == 2:
+            set_first()
+        wkv[:, :HD] = w_all[1, sx].reshape(512, HD)
+        wkv[:, HD:] = w_all[2, sx].reshape(512, HD)
+        features = pl.ds(pl.multiple_of(512 * sx, 512), 512)
+
+        def add_to(n):
+            run = pl.ds(pl.multiple_of(n * 512, 512), 512)
+            part = jnp.dot(waves[run, features], wkv[...], preferred_element_type=F32)
+            products[run, :] = part if d == 0 else products[run, :] + part
+
+        each(0, 4, add_to)
+        part = jnp.dot(table_ref[:, features], wkv[...], preferred_element_type=F32)
+        table_w[...] = part if d == 0 else table_w[...] + part
+    high = table_w[...].astype(BF)
+    tw[0] = high
+    tw[1] = (table_w[...] - high.astype(F32)).astype(BF)
 
     def keys_of(n):
         run = pl.ds(pl.multiple_of(n * 512, 512), 512)
-        both = jnp.dot(waves[run, :], wkv[...], preferred_element_type=F32)
-        both = both + jnp.dot(one_hot[run, :], tw[0], preferred_element_type=F32)
+        both = products[run, :] + jnp.dot(one_hot[run, :], tw[0], preferred_element_type=F32)
         both = both + jnp.dot(one_hot[run, :], tw[1], preferred_element_type=F32)
         both = (both * inverse[run, :]).astype(BF)
         keys[run, :] = both[:, :HD]
@@ -471,12 +496,12 @@
     own2[...] = second.astype(BF)
     spread2 = Exchange(own2, all_rows2, s_a2, r_a2, p, head_of, 16, whole=True)
     spread2.start()
+    hand_over(1)
 
     spread2.wait_all()
     ends.append(spread2.wait_sent)
 
     rows_normed(all_rows2)
-    hand_over(1)
     receive(0)
     hidden = []
     for i in range(4):
@@ -571,7 +596,8 @@
             pltpu.VMEM((4, 3, 32, HD), BF),
             pltpu.VMEM((3, 4, 4, 4, 32, HD), BF),
             pltpu.VMEM((4, 4, 4, 4, 128), jnp.int32),
-            pltpu.VMEM((D, 2 * HD), BF),
+            pltpu.VMEM((512, 2 * HD), BF),
+            pltpu.VMEM((256, 2 * HD), F32),
             pltpu.VMEM((2, 256, 2 * HD), BF),
             pltpu.VMEM((56, D), F32),
             pltpu.VMEM((56, D), F32),
@@ -610,12 +636,12 @@
             pltpu.VMEM((16, 16, 512), BF),
             pltpu.VMEM((16, 16, 512), BF),
             dma((3,)),
-            dma((2, 4)),
-            dma((2, 4)),
-            dma((2, 8)),
-            dma((2, 8)),
-            dma((2, 8)),
-            dma((2, 8)),
+            dma((3, 4)),
+            dma((3, 4)),
+            dma((3, 8)),
+            dma((3, 8)),
+            dma((3, 8)),
+            dma((3, 8)),
         ]
         + [dma((16,))] * 18
         + [dma((2,)), dma((2,)), dma((2,)), dma((2, 4)), dma((2, 4)), dma((2, 4)), dma((2, 4))],

time: 121 us -> 126 us (1.041)
  Pallas kernels: 119 us -> 123 us
    pallas_call x1, Pallas kernels: 119 us -> 123 us  [per_device(): pl.pallas_call(whole_kernel, out_shape=jax.ShapeDtypeStruct((4, D), F32),...]
where the time goes in v4:
time: 126 us; the launch traced here: 125 us
  Pallas kernels  123 us (98%)
  other arithmetic  1.37 us (1%)
    pallas_call x1, Pallas kernels, per_device(): pl.pallas_call(whole_kernel, out_shape=jax.ShapeDtypeStruct((4, D), F32),...  123 us

profile of v4, /device:TPU:1, one launch (start us, length us, event | category | flops | bytes accessed | tf_op | source)
XLA Modules:
  0.0 125.5 jit_solution(12192723774540256370)
XLA Ops:
  0.7 123.5 %shard_map.100 = f32[4,2048]{1,0:T(4,128)} custom-call(s32[1]{0:T(128)S(6)} %copy.11.offset_ref, s32[4,128]{1,0:T(4,128)} %bitcast.3, bf16[256,2048]{1,0:T(8,128)(2,1)} %table_ref.1, bf16[32,512]{1,0:T(8,128)(2,1)} %q_ref.1, bf16[2,32,512]{2,1,0:T(8,128)(2,1)} %kv_ref.1, bf16[512,2048]{1,0:T(8,128)(2,1)} %cout_ref.1, bf16[3,2048,512]{2,1,0:T(8,128)(2,1)} %sqkv_ref.1, ...), custom_call_target="tpu_custom_call" | custom-call | tf_op jit(solution)/shard_map/pallas_call | solution.py:590
  124.1 1.4 %convert_bitcast_fusion = bf16[1,4,2048]{2,1,0:T(4,128)(2,1)} fusion(f32[4,2048]{1,0:T(4,128)} %shard_map.100), kind=kLoop, calls=%fused_computation | loop fusion | flops 8192 | bytes 49152 | tf_op jit(solution)/shard_map/broadcast_in_dim | solution.py:655

commit v5 on v3

--- a/solution.py
+++ b/solution.py
@@ -88,10 +88,10 @@
 
 
 def whole_kernel(
-    offset_ref, tok_ref, table_ref, q_ref, kv_ref,
-    cout_ref, sqkv_ref, sout_ref, in_ref, mout_ref,
+    offset_ref, tok_ref, q_ref, kv_ref,
+    table_hbm, cout_ref, sqkv_ref, sout_ref, in_ref, mout_ref,
     out_ref,
-    stage, w_all, tokens, wkv, tw, sin_ref, cos_ref, rows_sin, rows_cos, waves, products, one_hot, inverse, latent, keys, values, q_own, q_all,
+    table_ref, stage, w_all, tokens, wkv, tw, sin_ref, cos_ref, rows_sin, rows_cos, waves, products, one_hot, inverse, latent, keys, values, q_own, q_all,
     o_msg, o_came, st_msg, st_came, w_co, w_qkv, w_so, msg, came, own, all_rows, normed, kv, kv_all, msg2, came2,
     own2, all_rows2, w_in, w_out, partial, msg3, came3,
     load, s1, r1, s2, r2, s3, r3, s_q, r_q, s_o, r_o, s_st, r_st, s_m, r_m, s_a, r_a, s_kv, r_kv, s_m2, r_m2,
@@ -119,7 +119,23 @@
     final_self = jnp.where(a == k, 4 * y + k, 16)
     sender_self = jnp.where(a == k, p, 16)
 
+    barrier = pltpu.get_barrier_semaphore()
+
+    def hello(device):
+        pl.semaphore_signal(barrier, inc=1, device_id=device, device_id_type=MESH)
+
+    each(1, 16, lambda i: hello(row_of((r + i) % 16)))
+    each(1, 16, lambda i: hello(head_of((p + i) % 16)))
+
+    def hello_sender(j):
+        @pl.when(j != sender_self)
+        def _():
+            hello(sender_of(j))
+
+    each(0, 16, hello_sender)
     row_at = pl.multiple_of(a * HD, HD)
+    table_load = pltpu.make_async_copy(table_hbm, table_ref, load.at[3])
+    table_load.start()
     loads = [
         pltpu.make_async_copy(cout_ref.at[pl.ds(row_at, HD), :], w_co, load.at[0]),
         pltpu.make_async_copy(sqkv_ref.at[:, :, pl.ds(row_at, HD)], w_qkv, load.at[1]),
@@ -127,59 +143,10 @@
     ]
     for copy in loads:
         copy.start()
-    barrier = pltpu.get_barrier_semaphore()
-
-    def hello(device):
-        pl.semaphore_signal(barrier, inc=1, device_id=device, device_id_type=MESH)
-
-    each(1, 16, lambda i: hello(row_of((r + i) % 16)))
-    each(1, 16, lambda i: hello(head_of((p + i) % 16)))
-
-    def hello_sender(j):
-        @pl.when(j != sender_self)
-        def _():
-            hello(sender_of(j))
-
-    each(0, 16, hello_sender)
     for h in range(4):
         stage[h, 0] = q_ref[:, 128 * h : 128 * h + 128]
         stage[h, 1] = kv_ref[0, :, 128 * h : 128 * h + 128]
         stage[h, 2] = kv_ref[1, :, 128 * h : 128 * h + 128]
-    offset = offset_ref[0]
-    index = lax.broadcasted_iota(jnp.int32, (56, 1), 0)
-    places = jnp.where(index < 4, 512 * (16 * x + 4 * index + k), offset + 256 * (index - 4) + 16 * r)
-    places = jnp.where(index < 8, places, jnp.where(index < 40, 16 * (index - 8), index - 40)).astype(F32)
-
-    def table_columns(j):
-        lanes = pl.ds(pl.multiple_of(j * 256, 256), 256)
-        pair = ((j * 256 + lax.broadcasted_iota(jnp.int32, (1, 256), 1)) // 2).astype(F32)
-        angles = places * jnp.exp(pair * (-2.0 * math.log(10000.0) / D))
-        sin_ref[:, lanes] = jnp.sin(angles)
-        cos_ref[:, lanes] = jnp.cos(angles)
-
-    each(0, 8, table_columns)
-    odd = lax.broadcasted_iota(jnp.int32, (1, D), 1) % 2 == 1
-    mid_sin, mid_cos = sin_ref[8:40], cos_ref[8:40]
-
-    def start_of(n):
-        s, co = sin_ref[pl.ds(n, 1)], cos_ref[pl.ds(n, 1)]
-        return jnp.where(odd, co, s), jnp.where(odd, -s, co)
-
-    def waves_of(n):
-        s, co = start_of(n)
-        rows_sin[...] = s * mid_cos + co * mid_sin
-        rows_cos[...] = co * mid_cos - s * mid_sin
-
-        def columns(j):
-            lanes = pl.ds(pl.multiple_of(j * 128, 128), 128)
-            low_sin, low_cos = sin_ref[40:56, lanes], cos_ref[40:56, lanes]
-            for m in range(32):
-                wave = rows_sin[m : m + 1, lanes] * low_cos + rows_cos[m : m + 1, lanes] * low_sin
-                waves[pl.ds(pl.multiple_of(n * 512 + 16 * m, 16), 16), lanes] = wave.astype(BF)
-
-        each(0, 16, columns)
-
-    each(0, 4, waves_of)
     pl.semaphore_wait(barrier, jnp.where(a == k, 45, 46))
     ends = []
 
@@ -197,22 +164,19 @@
     for part in range(3):
         w_all[part, x, a, k] = stage[a, part]
 
-    square = table_ref[...].astype(F32)
-    square = square * square
-    high = square.astype(BF)
-    lower = (square - high.astype(F32)).astype(BF)
-    ones = jnp.ones((8, D), BF)
-    across = (((1,), (1,)), ((), ()))
-    norms = lax.dot_general(ones, high, across, preferred_element_type=F32) + lax.dot_general(
-        ones, lower, across, preferred_element_type=F32
-    )
-    norms = norms[0:1]
-
-    def products_of(n):
-        run = pl.ds(pl.multiple_of(n * 512, 512), 512)
-        products[run, :] = lax.dot_general(waves[run, :], table_ref[...], across, preferred_element_type=F32)
-
-    each(0, 4, products_of)
+    offset = offset_ref[0]
+    index = lax.broadcasted_iota(jnp.int32, (56, 1), 0)
+    places = jnp.where(index < 4, 512 * (16 * x + 4 * index + k), offset + 256 * (index - 4) + 16 * r)
+    places = jnp.where(index < 8, places, jnp.where(index < 40, 16 * (index - 8), index - 40)).astype(F32)
+
+    def table_columns(j):
+        lanes = pl.ds(pl.multiple_of(j * 256, 256), 256)
+        pair = ((j * 256 + lax.broadcasted_iota(jnp.int32, (1, 256), 1)) // 2).astype(F32)
+        angles = places * jnp.exp(pair * (-2.0 * math.log(10000.0) / D))
+        sin_ref[:, lanes] = jnp.sin(angles)
+        cos_ref[:, lanes] = jnp.cos(angles)
+
+    each(0, 8, table_columns)
 
     for h in heads:
         arrive(tokens.at[x, h, k], r1.at[1, h], partner)
@@ -240,22 +204,46 @@
         copy.start()
         ends.append(copy.wait_send)
 
-    main = c == y // 2
-    source = jnp.logical_and(main, b == y % 2)
-    beside = at(x, a, 1 - b, c, y)
-    mine = [
-        pltpu.make_async_copy(in_ref, w_in.at[x], own_w.at[0]),
-        pltpu.make_async_copy(mout_ref, w_out.at[x], own_w.at[1]),
-    ]
-    step1 = [
-        push(in_ref, w_in.at[x], sw1.at[0], rw1.at[0], beside),
-        push(mout_ref, w_out.at[x], sw1.at[1], rw1.at[1], beside),
-    ]
-
-    @pl.when(source)
-    def _():
-        for copy in step1 + mine:
-            copy.start()
+    odd = lax.broadcasted_iota(jnp.int32, (1, D), 1) % 2 == 1
+    mid_sin, mid_cos = sin_ref[8:40], cos_ref[8:40]
+
+    def start_of(n):
+        s, co = sin_ref[pl.ds(n, 1)], cos_ref[pl.ds(n, 1)]
+        return jnp.where(odd, co, s), jnp.where(odd, -s, co)
+
+    def waves_of(n):
+        s, co = start_of(n)
+        rows_sin[...] = s * mid_cos + co * mid_sin
+        rows_cos[...] = co * mid_cos - s * mid_sin
+
+        def columns(j):
+            lanes = pl.ds(pl.multiple_of(j * 128, 128), 128)
+            low_sin, low_cos = sin_ref[40:56, lanes], cos_ref[40:56, lanes]
+            for m in range(32):
+                wave = rows_sin[m : m + 1, lanes] * low_cos + rows_cos[m : m + 1, lanes] * low_sin
+                waves[pl.ds(pl.multiple_of(n * 512 + 16 * m, 16), 16), lanes] = wave.astype(BF)
+
+        each(0, 16, columns)
+
+    each(0, 4, waves_of)
+
+    table_load.wait()
+    square = table_ref[...].astype(F32)
+    square = square * square
+    high = square.astype(BF)
+    lower = (square - high.astype(F32)).astype(BF)
+    ones = jnp.ones((8, D), BF)
+    across = (((1,), (1,)), ((), ()))
+    norms = lax.dot_general(ones, high, across, preferred_element_type=F32) + lax.dot_general(
+        ones, lower, across, preferred_element_type=F32
+    )
+    norms = norms[0:1]
+
+    def products_of(n):
+        run = pl.ds(pl.multiple_of(n * 512, 512), 512)
+        products[run, :] = lax.dot_general(waves[run, :], table_ref[...], across, preferred_element_type=F32)
+
+    each(0, 4, products_of)
 
     vocab = lax.broadcasted_iota(jnp.int32, (128, 256), 1).astype(F32)
     diagonal = lax.broadcasted_iota(jnp.int32, (128, 128), 0) == lax.broadcasted_iota(jnp.int32, (128, 128), 1)
@@ -312,6 +300,24 @@
     asked.start()
     ends.append(asked.wait_sent)
 
+    main = c == y // 2
+    source = jnp.logical_and(main, b == y % 2)
+    beside = at(x, a, 1 - b, c, y)
+    mine = [
+        pltpu.make_async_copy(in_ref, w_in.at[x], own_w.at[0]),
+        pltpu.make_async_copy(mout_ref, w_out.at[x], own_w.at[1]),
+    ]
+    step1 = [
+        push(in_ref, w_in.at[x], sw1.at[0], rw1.at[0], beside),
+        push(mout_ref, w_out.at[x], sw1.at[1], rw1.at[1], beside),
+    ]
+
+    @pl.when(source)
+    def _():
+        for copy in step1 + mine:
+            copy.start()
+
+
     wkv[:, :HD] = weights_of[1]
     wkv[:, HD:] = weights_of[2]
     table_w = jnp.dot(table_ref[...], wkv[...], preferred_element_type=F32)
@@ -403,8 +409,6 @@
             for i in range(4):
                 arrive(halves[h].at[i], rw3.at[h, i], partner)
 
-    set_out(0)
-
     maxima, totals = st_came[:, 0, :], st_came[:, 1, :]
     factor = jnp.exp(maxima - jnp.max(maxima, axis=0, keepdims=True))
     factor = factor / jnp.sum(factor * totals, axis=0, keepdims=True)
@@ -429,6 +433,7 @@
     shares(attended.astype(BF), w_co, msg)
     summed = Exchange(msg, came, s_m, r_m, p, head_of, 16)
     summed.start()
+    set_out(0)
     own_block = (pl.ds(pl.multiple_of(16 * y, 16), 16), pl.ds(pl.multiple_of(512 * a, 512), 512))
     own_latent = latent[own_block].astype(F32)
     summed.wait_all()
@@ -437,6 +442,7 @@
     own[...] = first.astype(BF)
     spread = Exchange(own, all_rows, s_a, r_a, p, head_of, 16, whole=True)
     spread.start()
+    set_out(1)
     spread.wait_all()
     ends.append(spread.wait_sent)
 
@@ -445,12 +451,11 @@
     kv[:, HD:] = jnp.dot(normed[...], w_qkv[2], preferred_element_type=F32).astype(BF)
     both = Exchange(kv, kv_all, s_kv, r_kv, r, row_of, 16, whole=True)
     both.start()
+    hand_over(0)
     query = jnp.dot(normed[...], w_qkv[0], preferred_element_type=F32).astype(BF)
     both.wait_all()
     ends.append(both.wait_sent)
 
-    set_out(1)
-    hand_over(0)
     all_keys = kv_all[:, :, :HD].reshape(LATENTS, HD)
     all_values = kv_all[:, :, HD:].reshape(LATENTS, HD)
     scores = lax.dot_general(query, all_keys, across, preferred_element_type=F32) * SCALE
@@ -465,6 +470,7 @@
     shares(attended.astype(BF), w_so, msg2)
     summed2 = Exchange(msg2, came2, s_m2, r_m2, p, head_of, 16)
     summed2.start()
+    hand_over(1)
     summed2.wait_all()
     ends.append(summed2.wait_sent)
     second = first + jnp.sum(came2[...].astype(F32), axis=0)
@@ -476,7 +482,6 @@
     ends.append(spread2.wait_sent)
 
     rows_normed(all_rows2)
-    hand_over(1)
     receive(0)
     hidden = []
     for i in range(4):
@@ -565,9 +570,10 @@
     rows = pl.pallas_call(
         whole_kernel,
         out_shape=jax.ShapeDtypeStruct((4, D), F32),
-        in_specs=[pl.BlockSpec(memory_space=pltpu.SMEM)] + [vmem] * 4 + [hbm] * 5,
+        in_specs=[pl.BlockSpec(memory_space=pltpu.SMEM)] + [vmem] * 3 + [hbm] * 6,
         out_specs=vmem,
         scratch_shapes=[
+            pltpu.VMEM((256, D), BF),
             pltpu.VMEM((4, 3, 32, HD), BF),
             pltpu.VMEM((3, 4, 4, 4, 32, HD), BF),
             pltpu.VMEM((4, 4, 4, 4, 128), jnp.int32),
@@ -609,7 +615,7 @@
             pltpu.VMEM((4, 64, 512), F32),
             pltpu.VMEM((16, 16, 512), BF),
             pltpu.VMEM((16, 16, 512), BF),
-            dma((3,)),
+            dma((4,)),
             dma((2, 4)),
             dma((2, 4)),
             dma((2, 8)),
@@ -623,8 +629,7 @@
             collective_id=0, has_side_effects=True, vmem_limit_bytes=VLIMIT
         ),
     )(
-        latent_offset, token_ids.reshape(4, 128), embed_table,
-        cross_q, cross_kv, cross_out, self_qkv, self_out, mlp_in, mlp_out,
+        latent_offset, token_ids.reshape(4, 128), cross_q, cross_kv, embed_table, cross_out, self_qkv, self_out, mlp_in, mlp_out,
     )
     return rows.astype(BF)[None]
 

time: 121 us -> 122 us (level)
    pallas_call x1, Pallas kernels: 119 us -> 120 us  [per_device(): pl.pallas_call(whole_kernel, out_shape=jax.ShapeDtypeStruct((4, D), F32),...]
where the time goes in v5:
time: 122 us
  Pallas kernels  120 us (98%)
  other arithmetic  1.37 us (1%)
    pallas_call x1, Pallas kernels, per_device(): pl.pallas_call(whole_kernel, out_shape=jax.ShapeDtypeStruct((4, D), F32),...  120 us

profile of v5, /device:TPU:1, one launch (start us, length us, event | category | flops | bytes accessed | tf_op | source)
XLA Modules:
  0.0 121.8 jit_solution(296539199087629809)
XLA Ops:
  0.7 119.8 %shard_map.100 = f32[4,2048]{1,0:T(4,128)} custom-call(s32[1]{0:T(128)S(6)} %copy.11.offset_ref, s32[4,128]{1,0:T(4,128)} %bitcast.3, bf16[32,512]{1,0:T(8,128)(2,1)} %q_ref.1, bf16[2,32,512]{2,1,0:T(8,128)(2,1)} %kv_ref.1, bf16[256,2048]{1,0:T(8,128)(2,1)} %table_hbm.1, bf16[512,2048]{1,0:T(8,128)(2,1)} %cout_ref.1, bf16[3,2048,512]{2,1,0:T(8,128)(2,1)} %sqkv_ref.1, ...), custom_call_target="tpu_custom_call" | custom-call | tf_op jit(solution)/shard_map/pallas_call | solution.py:570
  120.5 1.4 %convert_bitcast_fusion = bf16[1,4,2048]{2,1,0:T(4,128)(2,1)} fusion(f32[4,2048]{1,0:T(4,128)} %shard_map.100), kind=kLoop, calls=%fused_computation | loop fusion | flops 8192 | bytes 49152 | tf_op jit(solution)/shard_map/broadcast_in_dim | solution.py:634

commit v6 on v5

--- a/solution.py
+++ b/solution.py
@@ -160,6 +160,23 @@
     for copy in first_copies:
         copy.start()
         ends.append(copy.wait_send)
+    main = c == y // 2
+    source = jnp.logical_and(main, b == y % 2)
+    beside = at(x, a, 1 - b, c, y)
+    mine = [
+        pltpu.make_async_copy(in_ref, w_in.at[x], own_w.at[0]),
+        pltpu.make_async_copy(mout_ref, w_out.at[x], own_w.at[1]),
+    ]
+    step1 = [
+        push(in_ref, w_in.at[x], sw1.at[0], rw1.at[0], beside),
+        push(mout_ref, w_out.at[x], sw1.at[1], rw1.at[1], beside),
+    ]
+
+    @pl.when(source)
+    def _():
+        for copy in step1 + mine:
+            copy.start()
+
     tokens[x, a, k] = tok_ref[...]
     for part in range(3):
         w_all[part, x, a, k] = stage[a, part]
@@ -300,24 +317,6 @@
     asked.start()
     ends.append(asked.wait_sent)
 
-    main = c == y // 2
-    source = jnp.logical_and(main, b == y % 2)
-    beside = at(x, a, 1 - b, c, y)
-    mine = [
-        pltpu.make_async_copy(in_ref, w_in.at[x], own_w.at[0]),
-        pltpu.make_async_copy(mout_ref, w_out.at[x], own_w.at[1]),
-    ]
-    step1 = [
-        push(in_ref, w_in.at[x], sw1.at[0], rw1.at[0], beside),
-        push(mout_ref, w_out.at[x], sw1.at[1], rw1.at[1], beside),
-    ]
-
-    @pl.when(source)
-    def _():
-        for copy in step1 + mine:
-            copy.start()
-
-
     wkv[:, :HD] = weights_of[1]
     wkv[:, HD:] = weights_of[2]
     table_w = jnp.dot(table_ref[...], wkv[...], preferred_element_type=F32)
@@ -442,7 +441,6 @@
     own[...] = first.astype(BF)
     spread = Exchange(own, all_rows, s_a, r_a, p, head_of, 16, whole=True)
     spread.start()
-    set_out(1)
     spread.wait_all()
     ends.append(spread.wait_sent)
 
@@ -470,13 +468,14 @@
     shares(attended.astype(BF), w_so, msg2)
     summed2 = Exchange(msg2, came2, s_m2, r_m2, p, head_of, 16)
     summed2.start()
-    hand_over(1)
+    set_out(1)
     summed2.wait_all()
     ends.append(summed2.wait_sent)
     second = first + jnp.sum(came2[...].astype(F32), axis=0)
     own2[...] = second.astype(BF)
     spread2 = Exchange(own2, all_rows2, s_a2, r_a2, p, head_of, 16, whole=True)
     spread2.start()
+    hand_over(1)
 
     spread2.wait_all()
     ends.append(spread2.wait_sent)

time: 122 us -> 117 us (0.959)
  Pallas kernels: 120 us -> 115 us
    pallas_call x1, Pallas kernels: 120 us -> 115 us  [per_device(): pl.pallas_call(whole_kernel, out_shape=jax.ShapeDtypeStruct((4, D), F32),...]
where the time goes in v6:
time: 117 us
  Pallas kernels  115 us (98%)
  other arithmetic  1.37 us (1%)
    pallas_call x1, Pallas kernels, per_device(): pl.pallas_call(whole_kernel, out_shape=jax.ShapeDtypeStruct((4, D), F32),...  115 us

profile of v6, /device:TPU:1, one launch (start us, length us, event | category | flops | bytes accessed | tf_op | source)
XLA Modules:
  0.0 117.2 jit_solution(6085264837181337102)
XLA Ops:
  0.7 115.2 %shard_map.100 = f32[4,2048]{1,0:T(4,128)} custom-call(s32[1]{0:T(128)S(6)} %copy.11.offset_ref, s32[4,128]{1,0:T(4,128)} %bitcast.3, bf16[32,512]{1,0:T(8,128)(2,1)} %q_ref.1, bf16[2,32,512]{2,1,0:T(8,128)(2,1)} %kv_ref.1, bf16[256,2048]{1,0:T(8,128)(2,1)} %table_hbm.1, bf16[512,2048]{1,0:T(8,128)(2,1)} %cout_ref.1, bf16[3,2048,512]{2,1,0:T(8,128)(2,1)} %sqkv_ref.1, ...), custom_call_target="tpu_custom_call" | custom-call | tf_op jit(solution)/shard_map/pallas_call | solution.py:569
  115.8 1.4 %convert_bitcast_fusion = bf16[1,4,2048]{2,1,0:T(4,128)(2,1)} fusion(f32[4,2048]{1,0:T(4,128)} %shard_map.100), kind=kLoop, calls=%fused_computation | loop fusion | flops 8192 | bytes 49152 | tf_op jit(solution)/shard_map/broadcast_in_dim | solution.py:633

commit v7 on v6

--- a/solution.py
+++ b/solution.py
@@ -198,28 +198,35 @@
     for h in heads:
         arrive(tokens.at[x, h, k], r1.at[1, h], partner)
         arrive(w_all.at[:, x, h, k], r1.at[0, h], partner)
-    second_copies = []
-    for rx, rb in rows:
-        there = at(rx, a, rb, c, y)
-        j = 2 * rx + rb
-        second_copies.append(push(tokens.at[x, :, k], tokens.at[x, :, k], s2.at[1, j], r2.at[1, j_me], there))
-        second_copies.append(push(w_all.at[:, x, :, k], w_all.at[:, x, :, k], s2.at[0, j], r2.at[0, j_me], there))
-    for copy in second_copies:
-        copy.start()
-        ends.append(copy.wait_send)
-
-    def onward(rx, rb):
-        j = 2 * rx + rb
-        k2 = 2 * rb + c
-        return [
-            push(tokens.at[rx, :, k2], tokens.at[rx, :, k2], s3.at[1, j], r3.at[1, j], partner),
-            push(w_all.at[:, rx, :, k2], w_all.at[:, rx, :, k2], s3.at[0, j], r3.at[0, j], partner),
-        ]
-
-    third_copies = onward(x, b)
-    for copy in third_copies:
-        copy.start()
-        ends.append(copy.wait_send)
+    def pieces(rx, rb, core):
+        k2 = 2 * rb + core
+        return tokens.at[rx, :, k2], w_all.at[:, rx, :, k2]
+
+    def send_on(block, there, send, recv, sent, landed):
+        for n, ref in enumerate(block):
+            copy = push(ref, ref, send.at[1 - n, sent], recv.at[1 - n, landed], there)
+            copy.start()
+            ends.append(copy.wait_send)
+
+    def beside_on(rx):
+        send_on(pieces(rx, b, c), at(x, a, 1 - b, c, y), s2, r2, 2 * rx + 1 - b, 2 * rx + b)
+
+    def partner_on(rx, rb):
+        send_on(pieces(rx, rb, c), partner, s3, r3, 2 * rx + rb, 2 * rx + rb)
+
+    for d in (1, 3, 2):
+        rx = (x + d) % 4
+        send_on(pieces(x, b, c), at(rx, a, b, c, y), s2, r2, 2 * rx + b, j_me)
+    beside_on(x)
+    partner_on(x, b)
+
+    def hand_on(rx, rb, further):
+        for n, ref in enumerate(pieces(rx, rb, c)):
+            arrive(ref, r2.at[1 - n, 2 * rx + rb], partner)
+        if further:
+            beside_on(rx)
+        partner_on(rx, rb)
+
 
     odd = lax.broadcasted_iota(jnp.int32, (1, D), 1) % 2 == 1
     mid_sin, mid_cos = sin_ref[8:40], cos_ref[8:40]
@@ -243,6 +250,9 @@
         each(0, 16, columns)
 
     each(0, 4, waves_of)
+    hand_on((x + 1) % 4, b, True)
+    hand_on((x + 3) % 4, b, True)
+    hand_on(x, 1 - b, False)
 
     table_load.wait()
     square = table_ref[...].astype(F32)
@@ -261,6 +271,9 @@
         products[run, :] = lax.dot_general(waves[run, :], table_ref[...], across, preferred_element_type=F32)
 
     each(0, 4, products_of)
+    hand_on((x + 2) % 4, b, True)
+    hand_on((x + 1) % 4, 1 - b, False)
+    hand_on((x + 3) % 4, 1 - b, False)
 
     vocab = lax.broadcasted_iota(jnp.int32, (128, 256), 1).astype(F32)
     diagonal = lax.broadcasted_iota(jnp.int32, (128, 128), 0) == lax.broadcasted_iota(jnp.int32, (128, 128), 1)
@@ -280,16 +293,7 @@
 
     each(0, 4, scales_of)
 
-    for rx, rb in rows:
-        sx, sb = (2 * x + 4 - rx) % 4, rb
-        j = 2 * sx + sb
-        k2 = 2 * sb + c
-        arrive(tokens.at[sx, :, k2], r2.at[1, j], partner)
-        arrive(w_all.at[:, sx, :, k2], r2.at[0, j], partner)
-        more = onward(sx, sb)
-        for copy in more:
-            copy.start()
-            ends.append(copy.wait_send)
+    hand_on((x + 2) % 4, 1 - b, False)
     for rx, rb in [(x, b)] + rows:
         j = 2 * rx + rb
         k3 = 2 * rb + 1 - c

time: 117 us -> 119 us (1.017)
  Pallas kernels: 115 us -> 117 us
    pallas_call x1, Pallas kernels: 115 us -> 117 us  [per_device(): pl.pallas_call(whole_kernel, out_shape=jax.ShapeDtypeStruct((4, D), F32),...]
where the time goes in v7:
time: 119 us
  Pallas kernels  117 us (98%)
  other arithmetic  1.37 us (1%)
    pallas_call x1, Pallas kernels, per_device(): pl.pallas_call(whole_kernel, out_shape=jax.ShapeDtypeStruct((4, D), F32),...  117 us

profile of v7, /device:TPU:1, one launch (start us, length us, event | category | flops | bytes accessed | tf_op | source)
XLA Modules:
  0.0 118.6 jit_solution(5278260777835509849)
XLA Ops:
  0.7 116.6 %shard_map.100 = f32[4,2048]{1,0:T(4,128)} custom-call(s32[1]{0:T(128)S(6)} %copy.11.offset_ref, s32[4,128]{1,0:T(4,128)} %bitcast.3, bf16[32,512]{1,0:T(8,128)(2,1)} %q_ref.1, bf16[2,32,512]{2,1,0:T(8,128)(2,1)} %kv_ref.1, bf16[256,2048]{1,0:T(8,128)(2,1)} %table_hbm.1, bf16[512,2048]{1,0:T(8,128)(2,1)} %cout_ref.1, bf16[3,2048,512]{2,1,0:T(8,128)(2,1)} %sqkv_ref.1, ...), custom_call_target="tpu_custom_call" | custom-call | tf_op jit(solution)/shard_map/pallas_call | solution.py:573
  117.3 1.4 %convert_bitcast_fusion = bf16[1,4,2048]{2,1,0:T(4,128)(2,1)} fusion(f32[4,2048]{1,0:T(4,128)} %shard_map.100), kind=kLoop, calls=%fused_computation | loop fusion | flops 8192 | bytes 49152 | tf_op jit(solution)/shard_map/broadcast_in_dim | solution.py:637

commit v8 on v6

--- a/solution.py
+++ b/solution.py
@@ -174,7 +174,7 @@
 
     @pl.when(source)
     def _():
-        for copy in step1 + mine:
+        for copy in step1[:1] + mine:
             copy.start()
 
     tokens[x, a, k] = tok_ref[...]
@@ -441,6 +441,11 @@
     own[...] = first.astype(BF)
     spread = Exchange(own, all_rows, s_a, r_a, p, head_of, 16, whole=True)
     spread.start()
+
+    @pl.when(source)
+    def _():
+        step1[1].start()
+
     spread.wait_all()
     ends.append(spread.wait_sent)
 

time: 117 us -> 113 us (0.966)
  Pallas kernels: 115 us -> 110 us
    pallas_call x1, Pallas kernels: 115 us -> 110 us  [per_device(): pl.pallas_call(whole_kernel, out_shape=jax.ShapeDtypeStruct((4, D), F32),...]
where the time goes in v8:
time: 113 us; the launch traced here: 112 us
  Pallas kernels  110 us (97%)
  other arithmetic  1.37 us (1%)
    pallas_call x1, Pallas kernels, per_device(): pl.pallas_call(whole_kernel, out_shape=jax.ShapeDtypeStruct((4, D), F32),...  110 us

profile of v8, /device:TPU:1, one launch (start us, length us, event | category | flops | bytes accessed | tf_op | source)
XLA Modules:
  0.0 112.4 jit_solution(17520383487605849965)
XLA Ops:
  0.7 110.4 %shard_map.100 = f32[4,2048]{1,0:T(4,128)} custom-call(s32[1]{0:T(128)S(6)} %copy.11.offset_ref, s32[4,128]{1,0:T(4,128)} %bitcast.3, bf16[32,512]{1,0:T(8,128)(2,1)} %q_ref.1, bf16[2,32,512]{2,1,0:T(8,128)(2,1)} %kv_ref.1, bf16[256,2048]{1,0:T(8,128)(2,1)} %table_hbm.1, bf16[512,2048]{1,0:T(8,128)(2,1)} %cout_ref.1, bf16[3,2048,512]{2,1,0:T(8,128)(2,1)} %sqkv_ref.1, ...), custom_call_target="tpu_custom_call" | custom-call | tf_op jit(solution)/shard_map/pallas_call | solution.py:574
  111.1 1.4 %convert_bitcast_fusion = bf16[1,4,2048]{2,1,0:T(4,128)(2,1)} fusion(f32[4,2048]{1,0:T(4,128)} %shard_map.100), kind=kLoop, calls=%fused_computation | loop fusion | flops 8192 | bytes 49152 | tf_op jit(solution)/shard_map/broadcast_in_dim | solution.py:638

commit v9 on v8

--- a/solution.py
+++ b/solution.py
@@ -174,7 +174,7 @@
 
     @pl.when(source)
     def _():
-        for copy in step1[:1] + mine:
+        for copy in mine:
             copy.start()
 
     tokens[x, a, k] = tok_ref[...]
@@ -432,7 +432,11 @@
     shares(attended.astype(BF), w_co, msg)
     summed = Exchange(msg, came, s_m, r_m, p, head_of, 16)
     summed.start()
-    set_out(0)
+
+    @pl.when(source)
+    def _():
+        step1[0].start()
+
     own_block = (pl.ds(pl.multiple_of(16 * y, 16), 16), pl.ds(pl.multiple_of(512 * a, 512), 512))
     own_latent = latent[own_block].astype(F32)
     summed.wait_all()
@@ -441,6 +445,7 @@
     own[...] = first.astype(BF)
     spread = Exchange(own, all_rows, s_a, r_a, p, head_of, 16, whole=True)
     spread.start()
+    set_out(0)
 
     @pl.when(source)
     def _():
@@ -454,7 +459,6 @@
     kv[:, HD:] = jnp.dot(normed[...], w_qkv[2], preferred_element_type=F32).astype(BF)
     both = Exchange(kv, kv_all, s_kv, r_kv, r, row_of, 16, whole=True)
     both.start()
-    hand_over(0)
     query = jnp.dot(normed[...], w_qkv[0], preferred_element_type=F32).astype(BF)
     both.wait_all()
     ends.append(both.wait_sent)
@@ -473,6 +477,7 @@
     shares(attended.astype(BF), w_so, msg2)
     summed2 = Exchange(msg2, came2, s_m2, r_m2, p, head_of, 16)
     summed2.start()
+    hand_over(0)
     set_out(1)
     summed2.wait_all()
     ends.append(summed2.wait_sent)

time: 113 us -> 119 us (1.053)
  Pallas kernels: 110 us -> 117 us
    pallas_call x1, Pallas kernels: 110 us -> 117 us  [per_device(): pl.pallas_call(whole_kernel, out_shape=jax.ShapeDtypeStruct((4, D), F32),...]
where the time goes in v9:
time: 119 us
  Pallas kernels  117 us (98%)
  other arithmetic  1.37 us (1%)
    pallas_call x1, Pallas kernels, per_device(): pl.pallas_call(whole_kernel, out_shape=jax.ShapeDtypeStruct((4, D), F32),...  117 us

profile of v9, /device:TPU:1, one launch (start us, length us, event | category | flops | bytes accessed | tf_op | source)
XLA Modules:
  0.0 118.7 jit_solution(9968979972685562713)
XLA Ops:
  0.7 116.7 %shard_map.100 = f32[4,2048]{1,0:T(4,128)} custom-call(s32[1]{0:T(128)S(6)} %copy.11.offset_ref, s32[4,128]{1,0:T(4,128)} %bitcast.3, bf16[32,512]{1,0:T(8,128)(2,1)} %q_ref.1, bf16[2,32,512]{2,1,0:T(8,128)(2,1)} %kv_ref.1, bf16[256,2048]{1,0:T(8,128)(2,1)} %table_hbm.1, bf16[512,2048]{1,0:T(8,128)(2,1)} %cout_ref.1, bf16[3,2048,512]{2,1,0:T(8,128)(2,1)} %sqkv_ref.1, ...), custom_call_target="tpu_custom_call" | custom-call | tf_op jit(solution)/shard_map/pallas_call | solution.py:579
  117.4 1.4 %convert_bitcast_fusion = bf16[1,4,2048]{2,1,0:T(4,128)(2,1)} fusion(f32[4,2048]{1,0:T(4,128)} %shard_map.100), kind=kLoop, calls=%fused_computation | loop fusion | flops 8192 | bytes 49152 | tf_op jit(solution)/shard_map/broadcast_in_dim | solution.py:643
